TPU v7x, 256 devices: a whole 4x4x8 slice. The times are simulated.
256 devices in a mesh: tp: 16 (over z, core), ep: 16 (over y, x).
Axes of the slice: x: 4, y: 4, z: 8, core: 2. Of those that a mesh axis runs over, the one named last changes fastest.
Arguments:
- context: bfloat16 [4096, 4096], P('ep', 'tp'), may hold values from -6 to 6
- out_weight: bfloat16 [4096, 4096], P('tp'), may hold values from -0.125 to 0.125
- residual: bfloat16 [4096, 4096], P('ep', 'tp'), may hold values from -20 to 20
- norm_gain: bfloat16 [4096], replicated, may hold values from 0.099609375 to 1.8984375
- router_weight: bfloat16 [64, 4096], replicated, may hold values from -0.09375 to 0.09375
- expert_ids: int32 [4096, 8], P('ep'), may hold values from 0 to 63, all different within a row; in each aligned block of 256 rows (0 to 255, 256 to 511, ...) at most 64 rows name the same one
- w_gate: bfloat16 [256, 4096, 384], P(('tp', 'ep')), may hold values from -0.09375 to 0.09375
- w_up: bfloat16 [256, 4096, 384], P(('tp', 'ep')), may hold values from -0.09375 to 0.09375
- w_down: bfloat16 [256, 384, 4096], P(('tp', 'ep')), may hold values from -0.15625 to 0.15625
Outputs:
- layer_out: bfloat16 [4096, 4096], P('ep', 'tp')
Inputs may be any that keep to these rules, and one draw needn't show every extreme that they name: `expert_ids`: each row names 8 different experts. In each aligned block of 256 rows (the rows of one index of ep) no expert is named by more than 64 rows, a bound that some block reaches.
All inputs are finite; a program needn't handle non-finite values.
Results may differ from a plain program's by a relative error of at most 0.008.
Values may be sent and summed in bfloat16 or wider, within the bound.
A program may use at most 128 MiB of HBM per device.

v0:
```python
import jax
import jax.numpy as jnp
from jax import lax
from jax.sharding import PartitionSpec as P

SPLIT = 4


epsilon = 1e-06


def expert_block(arrivals, gate_weight, up_weight, down_weight):
    flat_rows = arrivals.reshape(-1, arrivals.shape[-1])
    gate_act = jnp.dot(flat_rows, gate_weight, preferred_element_type=jnp.float32)
    up_act = jnp.dot(flat_rows, up_weight, preferred_element_type=jnp.float32)
    hidden = (jax.nn.silu(gate_act) * up_act).astype(jnp.bfloat16)
    partial_value = jnp.dot(hidden, down_weight, preferred_element_type=jnp.float32).astype(
        jnp.bfloat16
    )
    return partial_value.reshape(arrivals.shape[:-1] + (down_weight.shape[1],))


def shards(
    context, out_weight, residual, norm_gain, router_weight, expert_ids, w_gate, w_up, w_down
):
    tp_count = lax.axis_size("tp")
    ep_count = lax.axis_size("ep")
    column_index = lax.axis_index("tp")
    share_width = residual.shape[1]
    model_width = share_width * tp_count
    tok_rows = residual.shape[0]
    attended = jnp.dot(context, out_weight, preferred_element_type=jnp.float32)
    gain_float = norm_gain.astype(jnp.float32)
    placed = lax.dynamic_update_slice(
        jnp.zeros_like(attended), residual.astype(jnp.float32), (0, column_index * share_width)
    )
    summed = lax.psum(attended + placed, "tp")
    state_float = lax.optimization_barrier(summed.astype(jnp.bfloat16)).astype(jnp.float32)
    inv_rms = lax.rsqrt(jnp.mean(state_float * state_float, axis=1, keepdims=True) + epsilon)
    normed = (state_float * inv_rms * gain_float).astype(jnp.bfloat16)
    state_share = lax.dynamic_slice_in_dim(state_float, column_index * share_width, share_width, 1)
    logits = lax.dot_general(
        normed, router_weight, (((1,), (1,)), ((), ())), preferred_element_type=jnp.float32
    )
    expert_count = router_weight.shape[0]
    route_count = expert_ids.shape[1]
    expert_range = lax.broadcasted_iota(jnp.int32, (1, 1, expert_count), 2)
    chosen = jnp.sum(
        jnp.where(expert_ids[:, :, None] == expert_range, logits[:, None, :], 0.0), axis=2
    )
    route_gates = jax.nn.softmax(chosen, axis=1)
    groups = ep_count // SPLIT
    column_experts = column_index * groups + lax.broadcasted_iota(jnp.int32, (1, 1, groups), 2)
    route_hit = expert_ids[:, :, None] == column_experts
    routed = jnp.sum(route_hit.astype(jnp.int32), axis=1)
    slot_of = jnp.cumsum(routed, axis=0) - 1
    capacity = min(tok_rows, 2 * tok_rows * route_count // expert_count)
    slot_ids = lax.broadcasted_iota(jnp.int32, (1, capacity, 1), 1)
    selector = ((slot_of.T[:, None, :] == slot_ids) & (routed.T[:, None, :] > 0)).astype(
        jnp.bfloat16
    )
    packed = jnp.einsum("qcr,rd->qcd", selector, normed, preferred_element_type=jnp.float32).astype(
        jnp.bfloat16
    )
    outgoing = jnp.repeat(packed, SPLIT, axis=0)
    partial_value = expert_block(
        lax.all_to_all(outgoing, "ep", split_axis=0, concat_axis=0, tiled=True),
        w_gate[0],
        w_up[0],
        w_down[0],
    )
    returned_rows = lax.all_to_all(partial_value, "ep", split_axis=0, concat_axis=0, tiled=True)
    column_gates = jnp.sum(jnp.where(route_hit, route_gates[:, :, None], 0.0), axis=1)
    summed_slices = jnp.sum(
        returned_rows.reshape(groups, SPLIT, capacity, model_width).astype(jnp.float32), axis=1
    )
    group_ids = lax.broadcasted_iota(jnp.int32, (1, groups), 1)
    gathered = summed_slices[group_ids, jnp.clip(slot_of, 0, capacity - 1)]
    mixture_column = jnp.sum(gathered * column_gates[:, :, None], axis=1)
    mixture_share = lax.psum_scatter(
        mixture_column.astype(jnp.bfloat16), "tp", scatter_dimension=1, tiled=True
    ).astype(jnp.float32)
    return (state_share + mixture_share).astype(jnp.bfloat16)


def solution(mesh):
    in_specs = (
        P("ep", "tp"),
        P("tp", None),
        P("ep", "tp"),
        P(),
        P(),
        P("ep", None),
        P(("tp", "ep"), None, None),
        P(("tp", "ep"), None, None),
        P(("tp", "ep"), None, None),
    )
    out_specs = P("ep", "tp")
    return jax.shard_map(shards, mesh=mesh, in_specs=in_specs, out_specs=out_specs, check_vma=False)
```

profile of v0, /device:TPU:32, one launch (start us, length us, event | category | flops | bytes accessed | tf_op | source)
XLA Modules:
  0.0 493.4 jit_solution(4469522311366918092)
XLA Ops:
  6.5 0.9 convert_element_type.47
  7.4 4.5 fusion.23
  11.9 1.7 add_dynamic-update-slice_fusion
  13.6 64.6 %all-reduce.1 = bf16[256,4096]{1,0:T(8,128)(2,1)} all-reduce(f32[256,4096]{1,0:T(8,128)} %add_dynamic-update-slice_fusion), channel_id=1, replica_groups=mesh['tp'=16,'ep'=16] {'tp'}, use_global_device_ids=true, to_apply=%region_0.0 | all-reduce | flops 1048576 | bytes 6291456 | tf_op jit(solution)/shard_map/psum | solution.py:37
  78.1 2.1 multiply_reduce_fusion.1
  80.4 1.2 reduce-window.6
  82.0 2.5 convolution_convert_fusion.1
  84.5 1.0 broadcast_in_dim.30
  85.6 100.6 %all_to_all.10 = bf16[16,64,4096]{2,1,0:T(8,128)(2,1)S(1)} all-to-all(bf16[16,64,4096]{2,1,0:T(8,128)(2,1)S(1)} %bitcast.44), channel_id=1, replica_groups=mesh['tp'=16,'ep'=16] {'ep'}, dimensions={0} | all-to-all | bytes 16777216 | tf_op jit(solution)/shard_map/all_to_all | solution.py:67
  186.2 4.5 fusion.3
  190.7 4.6 multiply_convert_fusion.1
  195.2 6.7 %convolution_convert_fusion = bf16[1024,4096]{1,0:T(8,128)(2,1)} fusion(bf16[1024,384]{1,0:T(8,128)(2,1)S(1)} %multiply_convert_fusion.1, bf16[1,384,4096]{2,1,0:T(8,128)(2,1)S(1)} %copy-done), kind=kOutput, calls=%fused_computation.3 | convolution fusion | flops 3225419776 | bytes 12320768 | tf_op jit(solution)/shard_map/dot_general | solution.py:17
  201.9 5.2 %all-to-all-start.1 = ((bf16[16,64,4096]{2,1,0:T(8,128)(2,1)}), bf16[16,64,4096]{2,1,0:T(8,128)(2,1)}, u32[]{:S(2)}, u32[]{:S(2)}) async-start(bf16[16,64,4096]{2,1,0:T(8,128)(2,1)} %bitcast.45), calls=%async_computation.1 | async-start | bytes 16777216 | tf_op jit(solution)/shard_map/all_to_all | solution.py:72
  207.1 0.1 copy.25
  207.5 0.8 fusion.8
  208.5 0.1 copy.24
  208.7 114.9 %all-to-all-done.1 = bf16[16,64,4096]{2,1,0:T(8,128)(2,1)} async-done(((bf16[16,64,4096]{2,1,0:T(8,128)(2,1)}), bf16[16,64,4096]{2,1,0:T(8,128)(2,1)}, u32[]{:S(2)}, u32[]{:S(2)}) %all-to-all-start.1) | async-done | bytes 8388640 | tf_op jit(solution)/shard_map/all_to_all | solution.py:72
  323.6 7.4 %convert_reduce_fusion = f32[4,64,4096]{2,1,0:T(8,128)} fusion(bf16[16,64,4096]{2,1,0:T(8,128)(2,1)} %all-to-all-done.1), kind=kLoop, calls=%fused_computation.1 | loop fusion | flops 7340032 | bytes 12582912 | tf_op jit(solution)/shard_map/reduce_sum | solution.py:74
  331.0 52.1 %gather_fusion = f32[1024,4096]{1,0:T(8,128)} fusion(f32[4,64,4096]{2,1,0:T(8,128)} %convert_reduce_fusion, s32[1024]{0:T(1024)S(1)} %reshape.93), kind=kCustom, calls=%fused_computation | custom fusion | bytes 33562624 | tf_op jit(solution)/shard_map/gather | solution.py:78
  383.1 19.0 %reshape.96 = f32[256,4,4096]{2,1,0:T(4,128)} reshape(f32[1024,4096]{1,0:T(8,128)} %gather_fusion) | data formatting | bytes 33554432 | tf_op jit(solution)/shard_map/gather | solution.py:78
  402.1 15.4 %multiply_reduce_fusion = bf16[256,4096]{1,0:T(8,128)(2,1)} fusion(f32[256,4,4096]{2,1,0:T(4,128)} %reshape.96, f32[256,4]{1,0:T(8,128)S(1)} %copy.24), kind=kLoop, calls=%fused_computation.2 | loop fusion | flops 7340032 | bytes 18878464 | tf_op jit(solution)/shard_map/reduce_sum | solution.py:79
  417.5 4.2 convert_element_type.45
  421.7 63.1 %reduce-scatter.2.cloned.1.call-done = bf16[256,256]{1,0:T(8,128)(2,1)} async-done(((bf16[256,4096]{1,0:T(8,128)(2,1)}), bf16[256,256]{1,0:T(8,128)(2,1)}) %reduce-scatter.2.cloned.1.call-update) | async-done | bytes 131088 | tf_op jit(solution)/shard_map/reduce_scatter | solution.py:80
  484.8 1.7 add_convert_fusion
  (37 shorter events, 1.0 us)
Async XLA Ops:
  6.5 188.7 %copy-start = (bf16[1,384,4096]{2,1,0:T(8,128)(2,1)S(1)}, bf16[1,384,4096]{2,1,0:T(8,128)(2,1)}, u32[]{:S(2)}) copy-start(bf16[1,384,4096]{2,1,0:T(8,128)(2,1)} %param.17) | copy-start | bytes 9437188
  6.5 5.3 %copy-start.3 = (bf16[256,256]{1,0:T(8,128)(2,1)S(1)}, bf16[256,256]{1,0:T(8,128)(2,1)}, u32[]{:S(2)}) copy-start(bf16[256,256]{1,0:T(8,128)(2,1)} %param.11) | copy-start | bytes 393220
  13.6 66.7 %copy-start.4 = (s32[256,8]{0,1:T(8,128)S(1)}, s32[256,8]{0,1:T(8,128)}, u32[]{:S(2)}) copy-start(s32[256,8]{0,1:T(8,128)} %param.14) | copy-start | bytes 24580
  85.5 100.6 %copy-start.5 = (bf16[1,4096,384]{2,1,0:T(8,128)(2,1)S(1)}, bf16[1,4096,384]{2,1,0:T(8,128)(2,1)}, u32[]{:S(2)}) copy-start(bf16[1,4096,384]{2,1,0:T(8,128)(2,1)} %param.15) | copy-start | bytes 9437188
  186.2 4.5 copy-start.6
  201.9 5.6 %copy-start.2 = (bf16[256,4096]{1,0:T(8,128)(2,1)S(1)}, bf16[256,4096]{1,0:T(8,128)(2,1)}, u32[]{:S(2)}) copy-start(bf16[256,4096]{1,0:T(8,128)(2,1)} %all-reduce.1) | copy-start | bytes 6291460
  201.9 5.6 %copy-start.7 = (bf16[64,4096]{1,0:T(8,128)(2,1)S(1)}, bf16[64,4096]{1,0:T(8,128)(2,1)}, u32[]{:S(2)}) copy-start(bf16[64,4096]{1,0:T(8,128)(2,1)} %param.13) | copy-start | bytes 1572868
  201.9 121.7 %all-to-all-start.1 = ((bf16[16,64,4096]{2,1,0:T(8,128)(2,1)}), bf16[16,64,4096]{2,1,0:T(8,128)(2,1)}, u32[]{:S(2)}, u32[]{:S(2)}) async-start(bf16[16,64,4096]{2,1,0:T(8,128)(2,1)} %bitcast.45), calls=%async_computation.1 | async-start | bytes 16777216 | tf_op jit(solution)/shard_map/all_to_all | solution.py:72
  207.1 277.7 %reduce-scatter.2.cloned.1.call-start = ((), (), s32[]{:S(2)}) async-start(), calls=%async_computation.3 | async-start | bytes 2228224 | tf_op jit(solution)/shard_map/reduce_scatter | solution.py:80
  417.5 69.0 %copy-start.1 = (bf16[1,384,4096]{2,1,0:T(8,128)(2,1)S(1)}, bf16[1,384,4096]{2,1,0:T(8,128)(2,1)}, u32[]{:S(2)}) copy-start(bf16[1,384,4096]{2,1,0:T(8,128)(2,1)} %param.17) | copy-start | bytes 9437188
Sparse Core Ops, SparseCore 0:
  417.7 67.0 reduce-scatter.1
where the time goes:
time: 499 us; the launch traced here: 493 us
  waiting for transfers between devices  178 us (36%)
  blocking collectives  165 us (33%)
  local copies, waits for them, and re-layouts  72.8 us (15%)
  other arithmetic  35.1 us (7%)
  matrix products  23.5 us (5%)
  between operations  13.5 us (3%)
  starting transfers between devices  5.22 us (1%)
    all_to_all x1, waiting for transfers between devices, shards(): lax.all_to_all(partial_value, 'ep', split_axis=0, concat_axis=0, tiled=True)  115 us
    all_to_all x1, blocking collectives, shards(): lax.all_to_all(outgoing, 'ep', split_axis=0, concat_axis=0, tiled=True)  101 us
    gather x2, local copies, waits for them, and re-layouts, shards(): gathered = summed_slices[group_ids, jnp.clip(slot_of, 0, capacity - 1)]  71.1 us
    psum x1, blocking collectives, shards(): summed = lax.psum(attended + placed, 'tp')  64.6 us
    reduce_scatter x1, waiting for transfers between devices, shards(): lax.psum_scatter(mixture_column.astype(jnp.bfloat16), 'tp', scatter_dimen...  63.1 us
    reduce_sum x1, other arithmetic, shards(): mixture_column = jnp.sum(gathered * column_gates[:, :, None], axis=1)  15.4 us
  transfers between devices with their start and end apart: 2, of which 2 were waited for; matrix products, arithmetic and copies ran while one was open for 1% of the time, Pallas kernels for 0%

commit v1 on v0

v1 whole, which is shorter than its diff:
```python
import functools

import jax
import jax.numpy as jnp
from jax import lax
from jax.experimental import pallas as pl
from jax.experimental.pallas import tpu as pltpu
from jax.sharding import PartitionSpec as P

SPLIT = 4
RING = 4
epsilon = 1e-06
MESH = pl.DeviceIdType.MESH
F32 = jnp.float32
BF16 = jnp.bfloat16
VMEM_BYTES = 58 * 2**20
DISTANCES = (4, 3, 5, 2, 6, 1, 7, 0)


def in_vmem(count):
    return [pl.BlockSpec(memory_space=pltpu.VMEM)] * count


def columns(index, width):
    return pl.ds(pl.multiple_of(index * width, width), width)


def greet(devices):
    barrier = pltpu.get_barrier_semaphore()
    for device in devices:
        pl.semaphore_signal(barrier, inc=1, device_id=device, device_id_type=MESH)
    pl.semaphore_wait(barrier, len(devices))


def remote(source, target, send, recv, device):
    return pltpu.make_async_remote_copy(
        src_ref=source, dst_ref=target, send_sem=send, recv_sem=recv, device_id=device, device_id_type=MESH
    )


def tp_place():
    tp, ep = lax.axis_index("tp"), lax.axis_index("ep")
    chips = lax.axis_size("tp") // 2
    z, core = tp // 2, tp % 2
    partner = (z * 2 + 1 - core, ep)
    right = (((z + 1) % chips) * 2 + core, ep)
    left = (((z + chips - 1) % chips) * 2 + core, ep)
    return z, core, chips, partner, right, left


def sum_scratch(rows, width):
    block = (rows, width)
    return [
        pltpu.VMEM((8, *block), BF16),
        pltpu.VMEM((8, *block), BF16),
        pltpu.VMEM((2, 4, *block), BF16),
        pltpu.VMEM((2, 4, *block), BF16),
        pltpu.SemaphoreType.DMA((8,)),
        pltpu.SemaphoreType.DMA((8,)),
        pltpu.SemaphoreType.DMA((2, 4)),
        pltpu.SemaphoreType.DMA((2, 4)),
    ]


def sum_over_tp(term, scratch):
    swap_out, swap_in, arm_out, arm_in, swap_send, swap_recv, arm_send, arm_recv = scratch
    z, core, chips, partner, right, left = tp_place()
    half = swap_out.shape[1] // 2
    whole = pl.ds(0, 2 * half)
    parts = (pl.ds(0, half), pl.ds(half, half))
    swaps = []
    for j in DISTANCES:
        block = ((z + j) % chips) * 2 + 1 - core
        swap_out[j] = term(block).astype(BF16)
        copy = remote(swap_out.at[j], swap_in.at[j], swap_send.at[j], swap_recv.at[j], partner)
        copy.start()
        swaps.append(copy)
    swaps = dict(zip(DISTANCES, swaps))

    def pair(j):
        mine = term(((z + j) % chips) * 2 + core)
        swaps[j].wait_recv()
        return mine + swap_in[j].astype(F32)

    sent = []

    def pass_on(arm, step, span):
        copy = remote(
            arm_out.at[arm, step, span],
            arm_in.at[arm, step, span],
            arm_send.at[arm, step],
            arm_recv.at[arm, step],
            (right, left)[arm],
        )
        copy.start()
        sent.append(copy)
        return copy

    far = pair(4)
    last = [None, None]
    for arm in range(2):
        arm_out[arm, 0, parts[arm]] = far[arm * half : (arm + 1) * half].astype(BF16)
        last[arm] = pass_on(arm, 0, parts[arm])
    for step in range(1, 4):
        for arm in range(2):
            mine = pair(4 - step if arm == 0 else 4 + step)
            last[arm].wait_recv()
            if step == 1:
                arm_out[arm, step] = mine.astype(BF16)
                span = parts[arm]
                came = arm_in[arm, 0, span].astype(F32)
                arm_out[arm, step, span] = (mine[arm * half : (arm + 1) * half] + came).astype(BF16)
            else:
                arm_out[arm, step] = (mine + arm_in[arm, step - 1].astype(F32)).astype(BF16)
            last[arm] = pass_on(arm, step, whole)
    total = pair(0)
    for arm in range(2):
        last[arm].wait_recv()
        total = total + arm_in[arm, 3].astype(F32)
    for copy in sent:
        copy.wait_send()
    for j in DISTANCES:
        swaps[j].wait_send()
    return total


def gather_over_tp(out, width, sems):
    right_send, right_recv, left_send, left_recv, near_send, near_recv = sems
    z, core, chips, partner, right, left = tp_place()
    half = out.shape[0] // 2
    whole = pl.ds(0, 2 * half)
    parts = (pl.ds(0, half), pl.ds(half, half))

    def at(j, span, side):
        return out.at[span, columns(((z + j + chips) % chips) * 2 + side, width)]

    copies = []

    def go(j, span, send, recv, device):
        ref = at(j, span, core)
        copy = remote(ref, ref, send, recv, device)
        copy.start()
        copies.append(copy)

    go(0, whole, right_send.at[0], right_recv.at[0], right)
    go(0, whole, left_send.at[0], left_recv.at[0], left)
    go(0, whole, near_send.at[0], near_recv.at[0], partner)
    for step in range(1, 5):
        span_r = parts[0] if step == 4 else whole
        span_l = parts[1] if step == 4 else whole
        ref = at(-step, span_r, core)
        remote(ref, ref, right_send.at[step - 1], right_recv.at[step - 1], right).wait_recv()
        if step < 4:
            go(-step, parts[0] if step == 3 else whole, right_send.at[step], right_recv.at[step], right)
            go(-step, whole, near_send.at[step], near_recv.at[step], partner)
        ref = at(step, span_l, core)
        remote(ref, ref, left_send.at[step - 1], left_recv.at[step - 1], left).wait_recv()
        if step < 4:
            go(step, parts[1] if step == 3 else whole, left_send.at[step], left_recv.at[step], left)
            go(step, whole, near_send.at[8 - step], near_recv.at[8 - step], partner)
    go(4, whole, near_send.at[4], near_recv.at[4], partner)
    for j in range(8):
        ref = at(-j, whole, 1 - core)
        remote(ref, ref, near_send.at[j], near_recv.at[j], partner).wait_recv()
    for copy in copies:
        copy.wait_send()


def attend_kernel(context, weight, residual, down, hidden, spread, *scratch):
    total_scratch, gather_sems, (spread_send, spread_recv) = scratch[:8], scratch[8:14], scratch[14:16]
    width = residual.shape[1]
    tp, ep = lax.axis_index("tp"), lax.axis_index("ep")
    y, x = ep // RING, ep % RING
    others = [(tp, y * RING + (x + k) % RING) for k in range(1, RING)]
    z, core, chips, partner, right, left = tp_place()
    greet([partner, right, left] + others)
    depth, quarter = down.shape[0], down.shape[1] // RING
    copies = []
    for k in range(1, RING):
        copy = remote(
            down.at[:, columns((x + k) % RING, quarter)],
            spread.at[pl.ds(k * depth, depth)],
            spread_send.at[k],
            spread_recv.at[k],
            others[k - 1],
        )
        copy.start()
        copies.append(copy)
    keep = pltpu.make_async_copy(down.at[:, columns(x, quarter)], spread.at[pl.ds(0, depth)], spread_send.at[0])
    keep.start()

    def term(block):
        return jnp.dot(context[...], weight[:, columns(block, width)], preferred_element_type=F32)

    total = sum_over_tp(term, total_scratch) + residual[...].astype(F32)
    hidden[:, columns(tp, width)] = total.astype(BF16)
    gather_over_tp(hidden, width, gather_sems)
    keep.wait()
    for copy in copies:
        copy.wait()


def attend(context, weight, residual, down):
    rows, width = residual.shape
    depth, model_width = down.shape
    return pl.pallas_call(
        attend_kernel,
        out_shape=(
            jax.ShapeDtypeStruct((rows, model_width), BF16),
            jax.ShapeDtypeStruct((RING * depth, model_width // RING), BF16),
        ),
        in_specs=in_vmem(3) + [pl.BlockSpec(memory_space=pl.ANY)],
        out_specs=(pl.BlockSpec(memory_space=pltpu.VMEM), pl.BlockSpec(memory_space=pl.ANY)),
        scratch_shapes=sum_scratch(rows, width)
        + [pltpu.SemaphoreType.DMA((4,))] * 4
        + [pltpu.SemaphoreType.DMA((8,))] * 2
        + [pltpu.SemaphoreType.DMA((4,))] * 2,
        compiler_params=pltpu.CompilerParams(
            collective_id=0, has_side_effects=True, vmem_limit_bytes=VMEM_BYTES
        ),
        name="attend",
    )(context, weight, residual, down)


def experts_kernel(packed, gate, up, down, back, rows, gate_up, spread, inner, out, *sems):
    (load, y_send, y_recv, right_send, right_recv, left_send, left_recv,
     far_send, far_recv, in_send, in_recv, out_send, out_recv) = sems
    tp, ep = lax.axis_index("tp"), lax.axis_index("ep")
    y, x = ep // RING, ep % RING
    slots = packed.shape[0] // RING
    width = packed.shape[1]
    block = RING * slots
    hidden_units = gate.shape[1]
    pieces = hidden_units // 128
    quarter = width // RING

    def device(dy, dx):
        return (tp, ((y + dy + RING) % RING) * RING + (x + dx + RING) % RING)

    greet([device(dy, dx) for dy in range(RING) for dx in range(RING) if dy or dx])

    def chunk(r, d):
        return pl.ds(r * block + d * slots, slots)

    y_copies = {}
    for d in (1, 3, 2):
        y_copies[d] = remote(packed.at[chunk(0, d)], rows.at[chunk(0, d)], y_send.at[d], y_recv.at[d], device(d, 0))
        y_copies[d].start()
    right, left = device(0, 1), device(0, -1)
    copies = []

    def to_sides(d, source):
        pair = (
            remote(source, rows.at[chunk(1, d)], right_send.at[d], right_recv.at[d], right),
            remote(source, rows.at[chunk(3, d)], left_send.at[d], left_recv.at[d], left),
        )
        for copy in pair:
            copy.start()
            copies.append(copy)
        return pair

    sides = {0: to_sides(0, packed.at[chunk(0, 0)])}
    loads = []
    for j in range(pieces):
        loads.append((gate.at[:, pl.ds(j * 128, 128)], gate_up.at[:, pl.ds(j * 256, 128)]))
        loads.append((up.at[:, pl.ds(j * 128, 128)], gate_up.at[:, pl.ds(j * 256 + 128, 128)]))
    loads.append((down, spread))
    loads.append((packed.at[chunk(0, 0)], rows.at[chunk(0, 0)]))
    loads = [pltpu.make_async_copy(a, b, load.at[i]) for i, (a, b) in enumerate(loads)]
    for copy in loads:
        copy.start()

    def y_arrived(d):
        y_copies[d].wait_recv()
        sides[d] = to_sides(d, rows.at[chunk(0, d)])

    def unit(r, h):
        span = pl.ds(r * block + h * 2 * slots, 2 * slots)

        def step(j, carry):
            both = jnp.dot(rows[span], gate_up[:, columns(j, 256)], preferred_element_type=F32)
            value, scale = both[:, :128], both[:, 128:]
            inner[span, columns(j, 128)] = (value / (1.0 + jnp.exp(-value)) * scale).astype(BF16)
            return carry

        lax.fori_loop(0, pieces, step, 0)
        for k in range(1, RING):
            there = (r + k) % RING
            copy = remote(
                inner.at[span, pl.ds(0, hidden_units)],
                inner.at[pl.ds(there * block + h * 2 * slots, 2 * slots), pl.ds(k * hidden_units, hidden_units)],
                in_send.at[r, h, k],
                in_recv.at[there, h, k],
                device(0, k),
            )
            copy.start()
            copies.append(copy)

    def came_right(d):
        sides[d][0].wait_recv()

    def came_left(d):
        sides[d][1].wait_recv()

    far = {}

    def onward(d):
        r = 1 if d % 2 == 0 else 3
        far[d] = remote(
            rows.at[chunk(r, d)],
            rows.at[chunk(2, d)],
            far_send.at[d],
            far_recv.at[d],
            right if r == 1 else left,
        )
        far[d].start()
        copies.append(far[d])

    def finish(r, h):
        span = pl.ds(r * block + h * 2 * slots, 2 * slots)
        for k in range(1, RING):
            ref = inner.at[span, pl.ds(k * hidden_units, hidden_units)]
            remote(ref, ref, in_send.at[r, h, k], in_recv.at[r, h, k], device(0, k)).wait_recv()

        def step(n, carry):
            out[span, columns(n, 256)] = jnp.dot(
                inner[span], spread[:, columns(n, 256)], preferred_element_type=F32
            ).astype(BF16)
            return carry

        lax.fori_loop(0, quarter // 256, step, 0)
        for d in (2 * h, 2 * h + 1):
            target = back.at[pl.ds(d * slots, slots), columns(x, quarter)]
            if r == 0 and d == 0:
                copy = pltpu.make_async_copy(out.at[chunk(0, 0)], target, out_send.at[0, 0])
            else:
                copy = remote(out.at[chunk(r, d)], target, out_send.at[r, d], out_recv.at[r, d], device(-d, -r))
            copy.start()
            if r == 0 and d == 0:
                own_back.append(copy)
            else:
                copies.append(copy)

    own_back = []
    y_arrived(1)
    for copy in loads:
        copy.wait()
    unit(0, 0)
    y_arrived(3)
    y_arrived(2)
    unit(0, 1)
    came_right(0)
    onward(0)
    came_left(0)
    came_left(1)
    onward(1)
    came_right(1)
    unit(1, 0)
    unit(3, 0)
    came_left(3)
    onward(3)
    came_right(3)
    came_right(2)
    onward(2)
    came_left(2)
    unit(1, 1)
    unit(3, 1)
    far[0].wait_recv()
    far[1].wait_recv()
    unit(2, 0)
    for r in (0, 1, 3, 2):
        finish(r, 0)
    far[2].wait_recv()
    far[3].wait_recv()
    unit(2, 1)
    for r in (0, 1, 3, 2):
        finish(r, 1)
    own_back[0].wait()
    for r in range(RING):
        for d in range(RING):
            if r or d:
                ref = back.at[pl.ds(d * slots, slots), columns((x + r) % RING, quarter)]
                remote(ref, ref, out_send.at[r, d], out_recv.at[r, d], device(d, r)).wait_recv()
    for copy in y_copies.values():
        copy.wait_send()
    for copy in copies:
        copy.wait_send()


def experts(packed, gate, up, down):
    total, width = packed.shape
    hidden_units = gate.shape[1]
    dma = pltpu.SemaphoreType.DMA
    return pl.pallas_call(
        experts_kernel,
        out_shape=jax.ShapeDtypeStruct((total, width), BF16),
        in_specs=in_vmem(1) + [pl.BlockSpec(memory_space=pl.ANY)] * 3,
        out_specs=pl.BlockSpec(memory_space=pltpu.VMEM),
        scratch_shapes=[
            pltpu.VMEM((RING * total, width), BF16),
            pltpu.VMEM((width, 2 * hidden_units), BF16),
            pltpu.VMEM((RING * hidden_units, width // RING), BF16),
            pltpu.VMEM((RING * total, RING * hidden_units), BF16),
            pltpu.VMEM((RING * total, width // RING), BF16),
            dma((hidden_units // 128 * 2 + 2,)),
        ]
        + [dma((RING,))] * 8
        + [dma((RING, 2, RING))] * 2
        + [dma((RING, RING))] * 2,
        compiler_params=pltpu.CompilerParams(
            collective_id=1, has_side_effects=True, vmem_limit_bytes=VMEM_BYTES
        ),
        name="experts",
    )(packed, gate, up, down)


def mix_kernel(gates, back, state, layer_out, *scratch):
    width = state.shape[1]
    z, core, chips, partner, right, left = tp_place()
    greet([partner, right, left])

    def term(block):
        return jnp.dot(gates[...], back[:, columns(block, width)], preferred_element_type=F32)

    layer_out[...] = (sum_over_tp(term, scratch) + state[...].astype(F32)).astype(BF16)


def mix(gates, back, state):
    rows, width = state.shape
    return pl.pallas_call(
        mix_kernel,
        out_shape=jax.ShapeDtypeStruct((rows, width), BF16),
        in_specs=in_vmem(3),
        out_specs=pl.BlockSpec(memory_space=pltpu.VMEM),
        scratch_shapes=sum_scratch(rows, width),
        compiler_params=pltpu.CompilerParams(
            collective_id=2, has_side_effects=True, vmem_limit_bytes=VMEM_BYTES
        ),
        name="mix",
    )(gates, back, state)


def route(hidden, norm_gain, router_weight, expert_ids, capacity):
    tp, ep = lax.axis_index("tp"), lax.axis_index("ep")
    y = ep // RING
    rows = hidden.shape[0]
    expert_count = router_weight.shape[0]
    state_float = hidden.astype(F32)
    inv_rms = lax.rsqrt(jnp.mean(state_float * state_float, axis=1, keepdims=True) + epsilon)
    normed = (state_float * inv_rms * norm_gain.astype(F32)).astype(BF16)
    logits = lax.dot_general(normed, router_weight, (((1,), (1,)), ((), ())), preferred_element_type=F32)
    every = lax.broadcasted_iota(jnp.int32, (1, 1, expert_count), 2)
    hit_all = jnp.any(expert_ids[:, :, None] == every, axis=1)
    top = jnp.max(jnp.where(hit_all, logits, -jnp.inf), axis=1, keepdims=True)
    raised = jnp.where(hit_all, jnp.exp(jnp.where(hit_all, logits - top, 0.0)), 0.0)
    gates_all = raised / jnp.sum(raised, axis=1, keepdims=True)
    mine = tp * RING + (y + lax.broadcasted_iota(jnp.int32, (1, 1, RING), 2)) % RING
    hit = jnp.any(expert_ids[:, :, None] == mine, axis=1)
    own_gates = jnp.sum(
        jnp.where(lax.broadcasted_iota(jnp.int32, (1, expert_count, 1), 1) == mine, gates_all[:, :, None], 0.0), axis=1
    )
    before = (
        lax.broadcasted_iota(jnp.int32, (rows, rows), 1) <= lax.broadcasted_iota(jnp.int32, (rows, rows), 0)
    ).astype(BF16)
    slot_of = jnp.dot(before, hit.astype(BF16), preferred_element_type=F32).astype(jnp.int32) - 1
    slots = lax.broadcasted_iota(jnp.int32, (1, 1, capacity), 2)
    chosen = (slot_of[:, :, None] == slots) & hit[:, :, None]
    selector = chosen.astype(BF16).reshape(rows, RING * capacity)
    gate_matrix = jnp.where(chosen, own_gates[:, :, None], 0.0).astype(BF16).reshape(rows, RING * capacity)
    packed = lax.dot_general(
        selector, normed, (((0,), (0,)), ((), ())), preferred_element_type=F32
    ).astype(BF16)
    return packed, gate_matrix


def shards(
    context, out_weight, residual, norm_gain, router_weight, expert_ids, w_gate, w_up, w_down
):
    tp = lax.axis_index("tp")
    rows, width = residual.shape
    hidden, spread_down = attend(context, out_weight, residual, w_down[0])
    capacity = min(rows, 2 * rows * expert_ids.shape[1] // router_weight.shape[0])
    packed, gate_matrix = route(hidden, norm_gain, router_weight, expert_ids, capacity)
    back = experts(packed, w_gate[0], w_up[0], spread_down)
    state = lax.dynamic_slice_in_dim(hidden, tp * width, width, 1)
    return mix(gate_matrix, back, state)


def solution(mesh):
    in_specs = (
        P("ep", "tp"),
        P("tp", None),
        P("ep", "tp"),
        P(),
        P(),
        P("ep", None),
        P(("tp", "ep"), None, None),
        P(("tp", "ep"), None, None),
        P(("tp", "ep"), None, None),
    )
    out_specs = P("ep", "tp")
    return jax.shard_map(shards, mesh=mesh, in_specs=in_specs, out_specs=out_specs, check_vma=False)
```

time: 499 us -> 243 us (0.49); the launches traced: 493 us -> 243 us
  Pallas kernels: 0 us -> 230 us
  waiting for transfers between devices: 178 us -> 0 us
  blocking collectives: 165 us -> 0 us
  local copies, waits for them, and re-layouts: 72.8 us -> 2.09 us
  other arithmetic: 35.1 us -> 5.6 us
  matrix products: 23.5 us -> 4.81 us
  between operations: 13.5 us -> 0.12 us
  starting transfers between devices: 5.22 us -> 0 us
    pallas_call x0 -> x3, Pallas kernels: none -> 230 us  [the longest x1 158 us: experts(): pl.pallas_call(experts_kernel, out_shape=jax.ShapeDtypeStruct((total, wid...]
    all_to_all x1 -> x0, waiting for transfers between devices: 115 us -> none  [shards(): lax.all_to_all(partial_value, 'ep', split_axis=0, concat_axis=0, tiled=True)]
    all_to_all x1 -> x0, blocking collectives: 101 us -> none  [shards(): lax.all_to_all(outgoing, 'ep', split_axis=0, concat_axis=0, tiled=True)]
    gather x2 -> x0, local copies, waits for them, and re-layouts: 71.1 us -> none  [shards(): gathered = summed_slices[group_ids, jnp.clip(slot_of, 0, capacity - 1)]]
    psum x1 -> x0, blocking collectives: 64.6 us -> none  [shards(): summed = lax.psum(attended + placed, 'tp')]
    reduce_scatter x1 -> x0, waiting for transfers between devices: 63.1 us -> none  [shards(): lax.psum_scatter(mixture_column.astype(jnp.bfloat16), 'tp', scatter_dimen...]
    reduce_sum x7 -> x3, other arithmetic: 25.2 us -> 2.39 us  [the longest x1 2.23 us: route(): jnp.mean(state_float * state_float, axis=1, keepdims=True) + epsilon]
    dot_general x6 -> x3, matrix products: 23.5 us -> 4.81 us  [the longest x1 2.42 us: route(): lax.dot_general(normed, router_weight, (((1,), (1,)), ((), ())), preferre...]
  transfers between devices with their start and end apart: 2 -> 0, of which waited for: 2 -> 0; matrix products, arithmetic and copies ran while one was open for 1% -> 0% of each run, Pallas kernels for 0% -> 0%
where the time goes in v1:
time: 243 us
  Pallas kernels  230 us (95%)
  other arithmetic  5.6 us (2%)
  matrix products  4.81 us (2%)
    pallas_call x1, Pallas kernels, experts(): pl.pallas_call(experts_kernel, out_shape=jax.ShapeDtypeStruct((total, wid...  158 us
    pallas_call x1, Pallas kernels, attend(): pl.pallas_call(attend_kernel, out_shape=(jax.ShapeDtypeStruct((rows, mode...  48.7 us
    pallas_call x1, Pallas kernels, mix(): pl.pallas_call(mix_kernel, out_shape=jax.ShapeDtypeStruct((rows, width),...  23.6 us

profile of v1, /device:TPU:32, one launch (start us, length us, event | category | flops | bytes accessed | tf_op | source)
XLA Modules:
  0.0 243.0 jit_solution(3979552843582064895)
XLA Ops:
  0.0 0.0 copy-start
  0.0 0.1 iota_compare_fusion.3
  0.1 0.8 compare_reduce_fusion
  0.9 0.1 eq.73
  1.0 0.2 fusion.3
  1.2 0.8 fusion.7
  2.0 0.7 convert_element_type.24
  2.7 0.1 copy.21
  2.9 0.1 copy.20
  3.0 48.7 %attend.1 = (bf16[256,4096]{1,0:T(8,128)(2,1)}, bf16[1536,1024]{1,0:T(8,128)(2,1)}) custom-call(bf16[256,256]{1,0:T(8,128)(2,1)} %context.1, bf16[256,4096]{1,0:T(8,128)(2,1)} %weight.1, bf16[256,256]{1,0:T(8,128)(2,1)} %residual.1, bf16[384,4096]{1,0:T(8,128)(2,1)} %bitcast.9), custom_call_target="tpu_custom_call" | custom-call | tf_op jit(solution)/shard_map/attend/pallas_call | solution.py:206
  51.7 0.0 copy-start.1
  51.7 2.2 fusion
  53.9 0.0 copy-done
  54.0 2.4 select_reduce_fusion.1
  56.5 0.1 select_reduce_fusion
  56.6 0.1 copy.22
  56.7 0.0 copy-done.1
  56.7 0.8 select_convert_fusion
  57.5 2.2 convolution_convert_fusion.packed
  59.7 158.1 %experts.1.back = bf16[256,4096]{1,0:T(8,128)(2,1)} custom-call(bf16[256,4096]{1,0:T(8,128)(2,1)} %convolution_convert_fusion.packed, bf16[4096,384]{1,0:T(8,128)(2,1)} %bitcast.10, bf16[4096,384]{1,0:T(8,128)(2,1)} %bitcast.11, bf16[1536,1024]{1,0:T(8,128)(2,1)} %get-tuple-element.8.down), custom_call_target="tpu_custom_call" | custom-call | tf_op jit(solution)/shard_map/experts/pallas_call | solution.py:394
  217.9 23.6 %mix.1 = bf16[256,256]{1,0:T(8,128)(2,1)} custom-call(bf16[256,256]{1,0:T(8,128)(2,1)} %get-tuple-element.9.gates, bf16[256,4096]{1,0:T(8,128)(2,1)} %experts.1.back, bf16[256,256]{1,0:T(8,128)(2,1)} %get-tuple-element.13.state), custom_call_target="tpu_custom_call" | custom-call | tf_op jit(solution)/shard_map/mix/pallas_call | solution.py:430
  241.4 1.6 copy.27
  (8 shorter events, 0.1 us)
Async XLA Ops:
  0.0 53.9 %copy-start = (bf16[64,4096]{1,0:T(8,128)(2,1)S(1)}, bf16[64,4096]{1,0:T(8,128)(2,1)}, u32[]{:S(2)}) copy-start(bf16[64,4096]{1,0:T(8,128)(2,1)} %param.13) | copy-start | bytes 1572868
  51.7 5.0 %copy-start.1 = (bf16[256,4096]{1,0:T(8,128)(2,1)S(1)}, bf16[256,4096]{1,0:T(8,128)(2,1)}, u32[]{:S(2)}) copy-start(bf16[256,4096]{1,0:T(8,128)(2,1)} %get-tuple-element.7) | copy-start | bytes 6291460

commit v2 on v1

--- a/solution.py
+++ b/solution.py
@@ -222,9 +222,9 @@
     )(context, weight, residual, down)
 
 
-def experts_kernel(packed, gate, up, down, back, rows, gate_up, spread, inner, out, *sems):
-    (load, y_send, y_recv, right_send, right_recv, left_send, left_recv,
-     far_send, far_recv, in_send, in_recv, out_send, out_recv) = sems
+def experts_kernel(packed, meta, gate, up, down, back, meta_all, rows, gate_up, spread, inner, out, *sems):
+    (load, y_send, y_recv, right_send, right_recv, left_send, left_recv, far_send, far_recv, meta_send, meta_recv,
+     in_send, in_recv, on_send, on_recv, out_send, out_recv) = sems
     tp, ep = lax.axis_index("tp"), lax.axis_index("ep")
     y, x = ep // RING, ep % RING
     slots = packed.shape[0] // RING
@@ -237,27 +237,35 @@
     def device(dy, dx):
         return (tp, ((y + dy + RING) % RING) * RING + (x + dx + RING) % RING)
 
-    greet([device(dy, dx) for dy in range(RING) for dx in range(RING) if dy or dx])
+    right, left = device(0, 1), device(0, -1)
+    greet([device(0, k) for k in range(1, RING)] + [device(k, 0) for k in range(1, RING)])
 
     def chunk(r, d):
         return pl.ds(r * block + d * slots, slots)
 
+    def unit_span(r, h):
+        return pl.ds(r * block + h * 2 * slots, 2 * slots)
+
+    def inner_columns(k):
+        return pl.ds(k * hidden_units, hidden_units)
+
+    copies = []
+
+    def send(source, target, send_sem, recv_sem, to):
+        copy = remote(source, target, send_sem, recv_sem, to)
+        copy.start()
+        copies.append(copy)
+        return copy
+
     y_copies = {}
     for d in (1, 3, 2):
-        y_copies[d] = remote(packed.at[chunk(0, d)], rows.at[chunk(0, d)], y_send.at[d], y_recv.at[d], device(d, 0))
-        y_copies[d].start()
-    right, left = device(0, 1), device(0, -1)
-    copies = []
+        y_copies[d] = send(packed.at[chunk(0, d)], rows.at[chunk(0, d)], y_send.at[d], y_recv.at[d], device(d, 0))
 
     def to_sides(d, source):
-        pair = (
-            remote(source, rows.at[chunk(1, d)], right_send.at[d], right_recv.at[d], right),
-            remote(source, rows.at[chunk(3, d)], left_send.at[d], left_recv.at[d], left),
+        return (
+            send(source, rows.at[chunk(1, d)], right_send.at[d], right_recv.at[d], right),
+            send(source, rows.at[chunk(3, d)], left_send.at[d], left_recv.at[d], left),
         )
-        for copy in pair:
-            copy.start()
-            copies.append(copy)
-        return pair
 
     sides = {0: to_sides(0, packed.at[chunk(0, 0)])}
     loads = []
@@ -266,16 +274,21 @@
         loads.append((up.at[:, pl.ds(j * 128, 128)], gate_up.at[:, pl.ds(j * 256 + 128, 128)]))
     loads.append((down, spread))
     loads.append((packed.at[chunk(0, 0)], rows.at[chunk(0, 0)]))
+    loads.append((meta, meta_all.at[pl.ds(0, 2 * RING)]))
     loads = [pltpu.make_async_copy(a, b, load.at[i]) for i, (a, b) in enumerate(loads)]
     for copy in loads:
         copy.start()
+    metas = [
+        send(meta, meta_all.at[pl.ds(k * 2 * RING, 2 * RING)], meta_send.at[k], meta_recv.at[k], device(0, k))
+        for k in range(1, RING)
+    ]
 
     def y_arrived(d):
         y_copies[d].wait_recv()
         sides[d] = to_sides(d, rows.at[chunk(0, d)])
 
     def unit(r, h):
-        span = pl.ds(r * block + h * 2 * slots, 2 * slots)
+        span = unit_span(r, h)
 
         def step(j, carry):
             both = jnp.dot(rows[span], gate_up[:, columns(j, 256)], preferred_element_type=F32)
@@ -284,17 +297,28 @@
             return carry
 
         lax.fori_loop(0, pieces, step, 0)
-        for k in range(1, RING):
+        for k in (1, 3):
             there = (r + k) % RING
-            copy = remote(
-                inner.at[span, pl.ds(0, hidden_units)],
-                inner.at[pl.ds(there * block + h * 2 * slots, 2 * slots), pl.ds(k * hidden_units, hidden_units)],
+            send(
+                inner.at[span, inner_columns(0)],
+                inner.at[unit_span(there, h), inner_columns(k)],
                 in_send.at[r, h, k],
                 in_recv.at[there, h, k],
                 device(0, k),
             )
-            copy.start()
-            copies.append(copy)
+
+    def relay(r, h):
+        for side, k in ((0, 1), (1, 3)):
+            here, there = (r + k) % RING, (r + 2) % RING
+            ref = inner.at[unit_span(here, h), inner_columns(k)]
+            remote(ref, ref, in_send.at[r, h, k], in_recv.at[here, h, k], right).wait_recv()
+            send(
+                inner.at[chunk(here, 2 * h + side), inner_columns(k)],
+                inner.at[chunk(there, 2 * h + side), inner_columns(2)],
+                on_send.at[r, h, side],
+                on_recv.at[there, h, side],
+                (right, left)[side],
+            )
 
     def came_right(d):
         sides[d][0].wait_recv()
@@ -306,21 +330,15 @@
 
     def onward(d):
         r = 1 if d % 2 == 0 else 3
-        far[d] = remote(
-            rows.at[chunk(r, d)],
-            rows.at[chunk(2, d)],
-            far_send.at[d],
-            far_recv.at[d],
-            right if r == 1 else left,
+        far[d] = send(
+            rows.at[chunk(r, d)], rows.at[chunk(2, d)], far_send.at[d], far_recv.at[d], right if r == 1 else left
         )
-        far[d].start()
-        copies.append(far[d])
 
     def finish(r, h):
-        span = pl.ds(r * block + h * 2 * slots, 2 * slots)
-        for k in range(1, RING):
-            ref = inner.at[span, pl.ds(k * hidden_units, hidden_units)]
-            remote(ref, ref, in_send.at[r, h, k], in_recv.at[r, h, k], device(0, k)).wait_recv()
+        span = unit_span(r, h)
+        for side in range(2):
+            ref = inner.at[chunk(r, 2 * h + side), inner_columns(2)]
+            remote(ref, ref, on_send.at[r, h, side], on_recv.at[r, h, side], right).wait_recv()
 
         def step(n, carry):
             out[span, columns(n, 256)] = jnp.dot(
@@ -330,25 +348,21 @@
 
         lax.fori_loop(0, quarter // 256, step, 0)
         for d in (2 * h, 2 * h + 1):
-            target = back.at[pl.ds(d * slots, slots), columns(x, quarter)]
-            if r == 0 and d == 0:
-                copy = pltpu.make_async_copy(out.at[chunk(0, 0)], target, out_send.at[0, 0])
+            target = back.at[chunk(r, d)]
+            if d == 0:
+                copy = pltpu.make_async_copy(out.at[chunk(r, 0)], target, out_send.at[r, 0])
+                copy.start()
+                kept.append(copy)
             else:
-                copy = remote(out.at[chunk(r, d)], target, out_send.at[r, d], out_recv.at[r, d], device(-d, -r))
-            copy.start()
-            if r == 0 and d == 0:
-                own_back.append(copy)
-            else:
-                copies.append(copy)
-
-    own_back = []
+                send(out.at[chunk(r, d)], target, out_send.at[r, d], out_recv.at[r, d], device(-d, 0))
+
+    kept = []
     y_arrived(1)
     for copy in loads:
         copy.wait()
     unit(0, 0)
     y_arrived(3)
     y_arrived(2)
-    unit(0, 1)
     came_right(0)
     onward(0)
     came_left(0)
@@ -357,6 +371,13 @@
     came_right(1)
     unit(1, 0)
     unit(3, 0)
+    relay(0, 0)
+    unit(0, 1)
+    relay(1, 0)
+    relay(3, 0)
+    far[0].wait_recv()
+    far[1].wait_recv()
+    unit(2, 0)
     came_left(3)
     onward(3)
     came_right(3)
@@ -365,79 +386,119 @@
     came_left(2)
     unit(1, 1)
     unit(3, 1)
-    far[0].wait_recv()
-    far[1].wait_recv()
-    unit(2, 0)
+    relay(2, 0)
+    relay(0, 1)
+    relay(1, 1)
+    relay(3, 1)
     for r in (0, 1, 3, 2):
         finish(r, 0)
     far[2].wait_recv()
     far[3].wait_recv()
     unit(2, 1)
+    relay(2, 1)
     for r in (0, 1, 3, 2):
         finish(r, 1)
-    own_back[0].wait()
+    for copy in kept:
+        copy.wait()
     for r in range(RING):
-        for d in range(RING):
-            if r or d:
-                ref = back.at[pl.ds(d * slots, slots), columns((x + r) % RING, quarter)]
-                remote(ref, ref, out_send.at[r, d], out_recv.at[r, d], device(d, r)).wait_recv()
-    for copy in y_copies.values():
-        copy.wait_send()
+        for d in range(1, RING):
+            ref = back.at[chunk(r, d)]
+            remote(ref, ref, out_send.at[r, d], out_recv.at[r, d], device(d, 0)).wait_recv()
+    for copy in metas:
+        copy.wait_recv()
     for copy in copies:
         copy.wait_send()
 
 
-def experts(packed, gate, up, down):
+def experts(packed, meta, gate, up, down):
     total, width = packed.shape
     hidden_units = gate.shape[1]
     dma = pltpu.SemaphoreType.DMA
     return pl.pallas_call(
         experts_kernel,
-        out_shape=jax.ShapeDtypeStruct((total, width), BF16),
-        in_specs=in_vmem(1) + [pl.BlockSpec(memory_space=pl.ANY)] * 3,
-        out_specs=pl.BlockSpec(memory_space=pltpu.VMEM),
+        out_shape=(
+            jax.ShapeDtypeStruct((RING * total, width // RING), BF16),
+            jax.ShapeDtypeStruct((RING * meta.shape[0], meta.shape[1]), F32),
+        ),
+        in_specs=in_vmem(2) + [pl.BlockSpec(memory_space=pl.ANY)] * 3,
+        out_specs=tuple(in_vmem(2)),
         scratch_shapes=[
             pltpu.VMEM((RING * total, width), BF16),
             pltpu.VMEM((width, 2 * hidden_units), BF16),
             pltpu.VMEM((RING * hidden_units, width // RING), BF16),
             pltpu.VMEM((RING * total, RING * hidden_units), BF16),
             pltpu.VMEM((RING * total, width // RING), BF16),
-            dma((hidden_units // 128 * 2 + 2,)),
+            dma((hidden_units // 128 * 2 + 3,)),
         ]
-        + [dma((RING,))] * 8
+        + [dma((RING,))] * 10
         + [dma((RING, 2, RING))] * 2
+        + [dma((RING, 2, 2))] * 2
         + [dma((RING, RING))] * 2,
         compiler_params=pltpu.CompilerParams(
             collective_id=1, has_side_effects=True, vmem_limit_bytes=VMEM_BYTES
         ),
         name="experts",
-    )(packed, gate, up, down)
-
-
-def mix_kernel(gates, back, state, layer_out, *scratch):
-    width = state.shape[1]
+    )(packed, meta, gate, up, down)
+
+
+def mix_kernel(meta, back, state, layer_out, share_out, share_in, matrix, share_send, share_recv, *scratch):
+    rows, width = state.shape
+    slots = back.shape[0] // RING // RING
+    tp, ep = lax.axis_index("tp"), lax.axis_index("ep")
+    y, x = ep // RING, ep % RING
     z, core, chips, partner, right, left = tp_place()
-    greet([partner, right, left])
+
+    def group_of(block):
+        return (block // RING - x + 2 + RING) % RING
+
+    target = (x * RING + tp % RING, y * RING + (x - group_of(tp) + RING) % RING)
+    from_x = tp // RING
+    shift = (from_x - x + RING) % RING
+    source = (((from_x + shift + 2) % RING) * RING + tp % RING, y * RING + from_x)
+    greet([partner, right, left, target, source])
+    place = lax.broadcasted_iota(jnp.int32, (slots, rows), 0).astype(F32)
+    for r in range(RING):
+        for d in range(RING):
+            slot = meta[pl.ds(r * 2 * RING + d, 1)]
+            gate = meta[pl.ds(r * 2 * RING + RING + d, 1)]
+            matrix[pl.ds((r * RING + d) * slots, slots)] = jnp.where(slot == place, gate, 0.0).astype(BF16)
 
     def term(block):
-        return jnp.dot(gates[...], back[:, columns(block, width)], preferred_element_type=F32)
-
-    layer_out[...] = (sum_over_tp(term, scratch) + state[...].astype(F32)).astype(BF16)
-
-
-def mix(gates, back, state):
+        span = pl.ds(pl.multiple_of(group_of(block) * RING * slots, RING * slots), RING * slots)
+        return lax.dot_general(
+            matrix[span],
+            back[span, columns(block % RING, width)],
+            (((0,), (0,)), ((), ())),
+            preferred_element_type=F32,
+        )
+
+    share_out[...] = sum_over_tp(term, scratch).astype(BF16)
+    copy = remote(share_out, share_in, share_send.at[0], share_recv.at[0], target)
+    copy.start()
+    copy.wait()
+    layer_out[...] = (share_in[...].astype(F32) + state[...].astype(F32)).astype(BF16)
+
+
+def mix(meta, back, state):
     rows, width = state.shape
     return pl.pallas_call(
         mix_kernel,
         out_shape=jax.ShapeDtypeStruct((rows, width), BF16),
         in_specs=in_vmem(3),
         out_specs=pl.BlockSpec(memory_space=pltpu.VMEM),
-        scratch_shapes=sum_scratch(rows, width),
+        scratch_shapes=[
+            pltpu.VMEM((rows, width), BF16),
+            pltpu.VMEM((rows, width), BF16),
+            pltpu.VMEM((back.shape[0], rows), BF16),
+            pltpu.SemaphoreType.DMA((1,)),
+            pltpu.SemaphoreType.DMA((1,)),
+        ]
+        + sum_scratch(rows, width),
         compiler_params=pltpu.CompilerParams(
             collective_id=2, has_side_effects=True, vmem_limit_bytes=VMEM_BYTES
         ),
         name="mix",
-    )(gates, back, state)
+    )(meta, back, state)
 
 
 def route(hidden, norm_gain, router_weight, expert_ids, capacity):
@@ -466,11 +527,12 @@
     slots = lax.broadcasted_iota(jnp.int32, (1, 1, capacity), 2)
     chosen = (slot_of[:, :, None] == slots) & hit[:, :, None]
     selector = chosen.astype(BF16).reshape(rows, RING * capacity)
-    gate_matrix = jnp.where(chosen, own_gates[:, :, None], 0.0).astype(BF16).reshape(rows, RING * capacity)
+    places = jnp.where(hit, slot_of, -1).astype(F32)
+    meta = jnp.concatenate([places, own_gates], axis=1).T
     packed = lax.dot_general(
         selector, normed, (((0,), (0,)), ((), ())), preferred_element_type=F32
     ).astype(BF16)
-    return packed, gate_matrix
+    return packed, meta
 
 
 def shards(
@@ -480,10 +542,10 @@
     rows, width = residual.shape
     hidden, spread_down = attend(context, out_weight, residual, w_down[0])
     capacity = min(rows, 2 * rows * expert_ids.shape[1] // router_weight.shape[0])
-    packed, gate_matrix = route(hidden, norm_gain, router_weight, expert_ids, capacity)
-    back = experts(packed, w_gate[0], w_up[0], spread_down)
+    packed, meta = route(hidden, norm_gain, router_weight, expert_ids, capacity)
+    back, meta_all = experts(packed, meta, w_gate[0], w_up[0], spread_down)
     state = lax.dynamic_slice_in_dim(hidden, tp * width, width, 1)
-    return mix(gate_matrix, back, state)
+    return mix(meta_all, back, state)
 
 
 def solution(mesh):

time: 243 us -> 237 us (0.975); the launches traced: 243 us -> 233 us
  Pallas kernels: 230 us -> 220 us
    pallas_call x1, Pallas kernels: 158 us -> 138 us  [experts(): pl.pallas_call(experts_kernel, out_shape=(jax.ShapeDtypeStruct((RING * to...]
    pallas_call x1, Pallas kernels: 23.6 us -> 33.7 us  [mix(): pl.pallas_call(mix_kernel, out_shape=jax.ShapeDtypeStruct((rows, width),...]
where the time goes in v2:
time: 237 us; the launch traced here: 233 us
  Pallas kernels  220 us (93%)
  other arithmetic  5.56 us (2%)
  matrix products  4.86 us (2%)
    pallas_call x1, Pallas kernels, experts(): pl.pallas_call(experts_kernel, out_shape=(jax.ShapeDtypeStruct((RING * to...  138 us
    pallas_call x1, Pallas kernels, attend(): pl.pallas_call(attend_kernel, out_shape=(jax.ShapeDtypeStruct((rows, mode...  48.7 us
    pallas_call x1, Pallas kernels, mix(): pl.pallas_call(mix_kernel, out_shape=jax.ShapeDtypeStruct((rows, width),...  33.7 us

profile of v2, /device:TPU:32, one launch (start us, length us, event | category | flops | bytes accessed | tf_op | source)
XLA Modules:
  0.0 233.2 jit_solution(10570337002492835325)
XLA Ops:
  0.0 0.0 copy-start
  0.0 0.1 iota_compare_fusion.3
  0.1 0.8 compare_reduce_fusion
  0.9 0.1 eq.72
  1.0 0.2 select_convert_fusion
  1.2 0.8 fusion.7
  2.0 0.7 convert_element_type.23
  2.7 0.1 fusion.8
  2.8 48.7 %attend.1 = (bf16[256,4096]{1,0:T(8,128)(2,1)}, bf16[1536,1024]{1,0:T(8,128)(2,1)}) custom-call(bf16[256,256]{1,0:T(8,128)(2,1)} %context.1, bf16[256,4096]{1,0:T(8,128)(2,1)} %weight.1, bf16[256,256]{1,0:T(8,128)(2,1)} %residual.1, bf16[384,4096]{1,0:T(8,128)(2,1)} %bitcast.14), custom_call_target="tpu_custom_call" | custom-call | tf_op jit(solution)/shard_map/attend/pallas_call | solution.py:206
  51.5 0.0 copy-start.1
  51.5 2.2 fusion
  53.7 0.0 copy-done
  53.7 2.4 %select_reduce_fusion.1 = (f32[256]{0:T(256)S(1)}, f32[256,64]{0,1:T(8,128)S(1)}) fusion(pred[256,64]{0,1:T(8,128)(4,1)S(1)} %fusion.7, bf16[64,4096]{1,0:T(8,128)(2,1)S(1)} %copy-done, bf16[256,4096]{1,0:T(8,128)(2,1)} %get-tuple-element.9, f32[4096]{0:T(1024)S(1)} %convert_element_type.23, f32[256]{0:T(256)S(1)} %add_rsqrt_fusion), kind=kOutput, calls=%fused_computation.16 | convolution fusion | flops 138444544 | bytes 2721792 | tf_op jit(solution)/shard_map/dot_general | solution.py:512
  56.2 0.1 select_reduce_fusion
  56.4 0.6 maximum_bitcast_fusion.meta
  57.0 0.0 copy-done.1
  57.0 0.7 constant_dynamic-slice_fusion.state
  57.6 2.3 convolution_convert_fusion.packed
  59.9 138.0 %experts.1 = (bf16[1024,1024]{1,0:T(8,128)(2,1)}, f32[32,256]{1,0:T(8,128)}) custom-call(bf16[256,4096]{1,0:T(8,128)(2,1)} %convolution_convert_fusion.packed, f32[8,256]{1,0:T(8,128)} %maximum_bitcast_fusion.meta, bf16[4096,384]{1,0:T(8,128)(2,1)} %bitcast.15, bf16[4096,384]{1,0:T(8,128)(2,1)} %bitcast.16, bf16[1536,1024]{1,0:T(8,128)(2,1)} %get-tuple-element.10.down), custom_call_target="tpu_custom_call" | custom-call | tf_op jit(solution)/shard_map/experts/pallas_call | solution.py:417
  197.9 33.7 %mix.1 = bf16[256,256]{1,0:T(8,128)(2,1)} custom-call(f32[32,256]{1,0:T(8,128)} %get-tuple-element.11.meta, bf16[1024,1024]{1,0:T(8,128)(2,1)} %get-tuple-element.12.back, bf16[256,256]{1,0:T(8,128)(2,1)} %constant_dynamic-slice_fusion.state), custom_call_target="tpu_custom_call" | custom-call | tf_op jit(solution)/shard_map/mix/pallas_call | solution.py:484
  231.6 1.6 copy.21
  (5 shorter events, 0.1 us)
Async XLA Ops:
  0.0 53.7 %copy-start = (bf16[64,4096]{1,0:T(8,128)(2,1)S(1)}, bf16[64,4096]{1,0:T(8,128)(2,1)}, u32[]{:S(2)}) copy-start(bf16[64,4096]{1,0:T(8,128)(2,1)} %param.13) | copy-start | bytes 1572868
  51.5 5.5 %copy-start.1 = (bf16[256,4096]{1,0:T(8,128)(2,1)S(1)}, bf16[256,4096]{1,0:T(8,128)(2,1)}, u32[]{:S(2)}) copy-start(bf16[256,4096]{1,0:T(8,128)(2,1)} %get-tuple-element.9) | copy-start | bytes 6291460

commit v3 on v2

--- a/solution.py
+++ b/solution.py
@@ -14,6 +14,8 @@
 F32 = jnp.float32
 BF16 = jnp.bfloat16
 VMEM_BYTES = 58 * 2**20
+PLACE = (3, 0, 2, 1)
+STAGES = ((1, 3), (2,), (0,))
 DISTANCES = (4, 3, 5, 2, 6, 1, 7, 0)
 
 
@@ -53,121 +55,118 @@
     return [
         pltpu.VMEM((8, *block), BF16),
         pltpu.VMEM((8, *block), BF16),
+        pltpu.VMEM((8, *block), F32),
         pltpu.VMEM((2, 4, *block), BF16),
         pltpu.VMEM((2, 4, *block), BF16),
         pltpu.SemaphoreType.DMA((8,)),
         pltpu.SemaphoreType.DMA((8,)),
-        pltpu.SemaphoreType.DMA((2, 4)),
-        pltpu.SemaphoreType.DMA((2, 4)),
+        pltpu.SemaphoreType.DMA((2, 4, 2)),
+        pltpu.SemaphoreType.DMA((2, 4, 2)),
     ]
 
 
-def sum_over_tp(term, scratch):
-    swap_out, swap_in, arm_out, arm_in, swap_send, swap_recv, arm_send, arm_recv = scratch
+def sum_over_tp(term, give, scratch):
+    swap_out, swap_in, pairs, arm_out, arm_in, swap_send, swap_recv, arm_send, arm_recv = scratch
     z, core, chips, partner, right, left = tp_place()
     half = swap_out.shape[1] // 2
-    whole = pl.ds(0, 2 * half)
-    parts = (pl.ds(0, half), pl.ds(half, half))
-    swaps = []
+    spans = (pl.ds(0, half), pl.ds(half, half))
+    swaps = {}
     for j in DISTANCES:
-        block = ((z + j) % chips) * 2 + 1 - core
-        swap_out[j] = term(block).astype(BF16)
-        copy = remote(swap_out.at[j], swap_in.at[j], swap_send.at[j], swap_recv.at[j], partner)
-        copy.start()
-        swaps.append(copy)
-    swaps = dict(zip(DISTANCES, swaps))
+        swap_out[j] = term(((z + j) % chips) * 2 + 1 - core).astype(BF16)
+        swaps[j] = remote(swap_out.at[j], swap_in.at[j], swap_send.at[j], swap_recv.at[j], partner)
+        swaps[j].start()
 
     def pair(j):
         mine = term(((z + j) % chips) * 2 + core)
         swaps[j].wait_recv()
-        return mine + swap_in[j].astype(F32)
-
-    sent = []
-
-    def pass_on(arm, step, span):
+        pairs[j] = mine + swap_in[j].astype(F32)
+
+    hops = {}
+
+    def hop(arm, h, step):
+        value = pairs[4 - step if arm == 0 else 4 + step, spans[h]]
+        if (arm, h, step - 1) in hops:
+            hops[arm, h, step - 1].wait_recv()
+            value = value + arm_in[arm, step - 1, spans[h]].astype(F32)
+        arm_out[arm, step, spans[h]] = value.astype(BF16)
         copy = remote(
-            arm_out.at[arm, step, span],
-            arm_in.at[arm, step, span],
-            arm_send.at[arm, step],
-            arm_recv.at[arm, step],
+            arm_out.at[arm, step, spans[h]],
+            arm_in.at[arm, step, spans[h]],
+            arm_send.at[arm, step, h],
+            arm_recv.at[arm, step, h],
             (right, left)[arm],
         )
         copy.start()
-        sent.append(copy)
-        return copy
-
-    far = pair(4)
-    last = [None, None]
-    for arm in range(2):
-        arm_out[arm, 0, parts[arm]] = far[arm * half : (arm + 1) * half].astype(BF16)
-        last[arm] = pass_on(arm, 0, parts[arm])
+        hops[arm, h, step] = copy
+
+    pair(4)
+    hop(0, 0, 0)
+    hop(1, 1, 0)
     for step in range(1, 4):
-        for arm in range(2):
-            mine = pair(4 - step if arm == 0 else 4 + step)
-            last[arm].wait_recv()
-            if step == 1:
-                arm_out[arm, step] = mine.astype(BF16)
-                span = parts[arm]
-                came = arm_in[arm, 0, span].astype(F32)
-                arm_out[arm, step, span] = (mine[arm * half : (arm + 1) * half] + came).astype(BF16)
-            else:
-                arm_out[arm, step] = (mine + arm_in[arm, step - 1].astype(F32)).astype(BF16)
-            last[arm] = pass_on(arm, step, whole)
-    total = pair(0)
-    for arm in range(2):
-        last[arm].wait_recv()
-        total = total + arm_in[arm, 3].astype(F32)
-    for copy in sent:
+        pair(4 - step)
+        pair(4 + step)
+        hop(0, 1, step)
+        hop(1, 0, step)
+        hop(0, 0, step)
+        hop(1, 1, step)
+    pair(0)
+    for h in range(2):
+        total = pairs[0, spans[h]]
+        for arm in (1 - h, h):
+            hops[arm, h, 3].wait_recv()
+            total = total + arm_in[arm, 3, spans[h]].astype(F32)
+        give(h, spans[h], total)
+    for copy in list(hops.values()) + list(swaps.values()):
         copy.wait_send()
-    for j in DISTANCES:
-        swaps[j].wait_send()
-    return total
 
 
 def gather_over_tp(out, width, sems):
-    right_send, right_recv, left_send, left_recv, near_send, near_recv = sems
+    arm_send, arm_recv, near_send, near_recv = sems
     z, core, chips, partner, right, left = tp_place()
     half = out.shape[0] // 2
-    whole = pl.ds(0, 2 * half)
-    parts = (pl.ds(0, half), pl.ds(half, half))
-
-    def at(j, span, side):
-        return out.at[span, columns(((z + j + chips) % chips) * 2 + side, width)]
-
     copies = []
 
-    def go(j, span, send, recv, device):
-        ref = at(j, span, core)
-        copy = remote(ref, ref, send, recv, device)
-        copy.start()
-        copies.append(copy)
-
-    go(0, whole, right_send.at[0], right_recv.at[0], right)
-    go(0, whole, left_send.at[0], left_recv.at[0], left)
-    go(0, whole, near_send.at[0], near_recv.at[0], partner)
-    for step in range(1, 5):
-        span_r = parts[0] if step == 4 else whole
-        span_l = parts[1] if step == 4 else whole
-        ref = at(-step, span_r, core)
-        remote(ref, ref, right_send.at[step - 1], right_recv.at[step - 1], right).wait_recv()
-        if step < 4:
-            go(-step, parts[0] if step == 3 else whole, right_send.at[step], right_recv.at[step], right)
-            go(-step, whole, near_send.at[step], near_recv.at[step], partner)
-        ref = at(step, span_l, core)
-        remote(ref, ref, left_send.at[step - 1], left_recv.at[step - 1], left).wait_recv()
-        if step < 4:
-            go(step, parts[1] if step == 3 else whole, left_send.at[step], left_recv.at[step], left)
-            go(step, whole, near_send.at[8 - step], near_recv.at[8 - step], partner)
-    go(4, whole, near_send.at[4], near_recv.at[4], partner)
-    for j in range(8):
-        ref = at(-j, whole, 1 - core)
-        remote(ref, ref, near_send.at[j], near_recv.at[j], partner).wait_recv()
-    for copy in copies:
-        copy.wait_send()
+    def at(j, h, side):
+        return out.at[pl.ds(h * half, half), columns(((z + j + chips) % chips) * 2 + side, width)]
+
+    def pass_on(arm, h, step):
+        ref = at(step if arm else -step, h, core)
+        copies.append(remote(ref, ref, arm_send.at[arm, step, h], arm_recv.at[arm, step, h], (right, left)[arm]))
+        copies[-1].start()
+
+    def to_partner(j, h):
+        ref = at(j, h, core)
+        copies.append(remote(ref, ref, near_send.at[j % 8, h], near_recv.at[j % 8, h], partner))
+        copies[-1].start()
+
+    def start(h):
+        for arm in (h, 1 - h):
+            pass_on(arm, h, 0)
+        to_partner(0, h)
+
+    def finish():
+        for step in range(1, 5):
+            for arm, h in ((0, 0), (1, 0), (1, 1), (0, 1)):
+                if step == 4 and arm != h:
+                    continue
+                j = step if arm else -step
+                ref = at(j, h, core)
+                remote(ref, ref, arm_send.at[arm, step - 1, h], arm_recv.at[arm, step - 1, h], right).wait_recv()
+                if step < 3 or (step == 3 and arm == h):
+                    pass_on(arm, h, step)
+                to_partner(j, h)
+        for j in range(8):
+            for h in range(2):
+                ref = at(j, h, 1 - core)
+                remote(ref, ref, near_send.at[j, h], near_recv.at[j, h], partner).wait_recv()
+        for copy in copies:
+            copy.wait_send()
+
+    return start, finish
 
 
 def attend_kernel(context, weight, residual, down, hidden, spread, *scratch):
-    total_scratch, gather_sems, (spread_send, spread_recv) = scratch[:8], scratch[8:14], scratch[14:16]
+    total_scratch, gather_sems, (spread_send, spread_recv) = scratch[:9], scratch[9:13], scratch[13:15]
     width = residual.shape[1]
     tp, ep = lax.axis_index("tp"), lax.axis_index("ep")
     y, x = ep // RING, ep % RING
@@ -192,9 +191,14 @@
     def term(block):
         return jnp.dot(context[...], weight[:, columns(block, width)], preferred_element_type=F32)
 
-    total = sum_over_tp(term, total_scratch) + residual[...].astype(F32)
-    hidden[:, columns(tp, width)] = total.astype(BF16)
-    gather_over_tp(hidden, width, gather_sems)
+    start, finish = gather_over_tp(hidden, width, gather_sems)
+
+    def give(h, span, total):
+        hidden[span, columns(tp, width)] = (total + residual[span].astype(F32)).astype(BF16)
+        start(h)
+
+    sum_over_tp(term, give, total_scratch)
+    finish()
     keep.wait()
     for copy in copies:
         copy.wait()
@@ -212,8 +216,8 @@
         in_specs=in_vmem(3) + [pl.BlockSpec(memory_space=pl.ANY)],
         out_specs=(pl.BlockSpec(memory_space=pltpu.VMEM), pl.BlockSpec(memory_space=pl.ANY)),
         scratch_shapes=sum_scratch(rows, width)
-        + [pltpu.SemaphoreType.DMA((4,))] * 4
-        + [pltpu.SemaphoreType.DMA((8,))] * 2
+        + [pltpu.SemaphoreType.DMA((2, 4, 2))] * 2
+        + [pltpu.SemaphoreType.DMA((8, 2))] * 2
         + [pltpu.SemaphoreType.DMA((4,))] * 2,
         compiler_params=pltpu.CompilerParams(
             collective_id=0, has_side_effects=True, vmem_limit_bytes=VMEM_BYTES
@@ -241,10 +245,14 @@
     greet([device(0, k) for k in range(1, RING)] + [device(k, 0) for k in range(1, RING)])
 
     def chunk(r, d):
-        return pl.ds(r * block + d * slots, slots)
+        return pl.ds(r * block + PLACE[d] * slots, slots)
 
     def unit_span(r, h):
-        return pl.ds(r * block + h * 2 * slots, 2 * slots)
+        return pl.ds(r * block + PLACE[STAGES[h][0]] * slots, len(STAGES[h]) * slots)
+
+    def half_span(r, h, side):
+        half = len(STAGES[h]) * slots // 2
+        return pl.ds(r * block + PLACE[STAGES[h][0]] * slots + side * half, half)
 
     def inner_columns(k):
         return pl.ds(k * hidden_units, hidden_units)
@@ -259,7 +267,7 @@
 
     y_copies = {}
     for d in (1, 3, 2):
-        y_copies[d] = send(packed.at[chunk(0, d)], rows.at[chunk(0, d)], y_send.at[d], y_recv.at[d], device(d, 0))
+        y_copies[d] = send(packed.at[pl.ds(d * slots, slots)], rows.at[chunk(0, d)], y_send.at[d], y_recv.at[d], device(d, 0))
 
     def to_sides(d, source):
         return (
@@ -267,13 +275,13 @@
             send(source, rows.at[chunk(3, d)], left_send.at[d], left_recv.at[d], left),
         )
 
-    sides = {0: to_sides(0, packed.at[chunk(0, 0)])}
+    sides = {0: to_sides(0, packed.at[pl.ds(0, slots)])}
     loads = []
     for j in range(pieces):
         loads.append((gate.at[:, pl.ds(j * 128, 128)], gate_up.at[:, pl.ds(j * 256, 128)]))
         loads.append((up.at[:, pl.ds(j * 128, 128)], gate_up.at[:, pl.ds(j * 256 + 128, 128)]))
     loads.append((down, spread))
-    loads.append((packed.at[chunk(0, 0)], rows.at[chunk(0, 0)]))
+    loads.append((packed.at[pl.ds(0, slots)], rows.at[chunk(0, 0)]))
     loads.append((meta, meta_all.at[pl.ds(0, 2 * RING)]))
     loads = [pltpu.make_async_copy(a, b, load.at[i]) for i, (a, b) in enumerate(loads)]
     for copy in loads:
@@ -313,8 +321,8 @@
             ref = inner.at[unit_span(here, h), inner_columns(k)]
             remote(ref, ref, in_send.at[r, h, k], in_recv.at[here, h, k], right).wait_recv()
             send(
-                inner.at[chunk(here, 2 * h + side), inner_columns(k)],
-                inner.at[chunk(there, 2 * h + side), inner_columns(2)],
+                inner.at[half_span(here, h, side), inner_columns(k)],
+                inner.at[half_span(there, h, side), inner_columns(2)],
                 on_send.at[r, h, side],
                 on_recv.at[there, h, side],
                 (right, left)[side],
@@ -328,16 +336,23 @@
 
     far = {}
 
-    def onward(d):
-        r = 1 if d % 2 == 0 else 3
-        far[d] = send(
-            rows.at[chunk(r, d)], rows.at[chunk(2, d)], far_send.at[d], far_recv.at[d], right if r == 1 else left
+    def onward(h, side):
+        far[h, side] = send(
+            rows.at[half_span((1, 3)[side], h, side)],
+            rows.at[half_span(2, h, side)],
+            far_send.at[h, side],
+            far_recv.at[h, side],
+            (right, left)[side],
         )
+
+    def came_far(h):
+        far[h, 0].wait_recv()
+        far[h, 1].wait_recv()
 
     def finish(r, h):
         span = unit_span(r, h)
         for side in range(2):
-            ref = inner.at[chunk(r, 2 * h + side), inner_columns(2)]
+            ref = inner.at[half_span(r, h, side), inner_columns(2)]
             remote(ref, ref, on_send.at[r, h, side], on_recv.at[r, h, side], right).wait_recv()
 
         def step(n, carry):
@@ -347,7 +362,7 @@
             return carry
 
         lax.fori_loop(0, quarter // 256, step, 0)
-        for d in (2 * h, 2 * h + 1):
+        for d in STAGES[h]:
             target = back.at[chunk(r, d)]
             if d == 0:
                 copy = pltpu.make_async_copy(out.at[chunk(r, 0)], target, out_send.at[r, 0])
@@ -358,46 +373,57 @@
 
     kept = []
     y_arrived(1)
+    y_arrived(3)
     for copy in loads:
         copy.wait()
     unit(0, 0)
-    y_arrived(3)
+    came_right(0)
+    came_left(0)
+    unit(0, 2)
     y_arrived(2)
-    came_right(0)
-    onward(0)
-    came_left(0)
+    came_right(1)
+    onward(0, 0)
+    came_left(3)
+    onward(0, 1)
     came_left(1)
-    onward(1)
-    came_right(1)
+    came_right(3)
     unit(1, 0)
     unit(3, 0)
     relay(0, 0)
+    unit(1, 2)
+    unit(3, 2)
     unit(0, 1)
+    came_right(2)
+    onward(1, 0)
+    came_left(2)
+    onward(1, 1)
     relay(1, 0)
     relay(3, 0)
-    far[0].wait_recv()
-    far[1].wait_recv()
+    came_far(0)
     unit(2, 0)
-    came_left(3)
-    onward(3)
-    came_right(3)
-    came_right(2)
-    onward(2)
-    came_left(2)
+    onward(2, 0)
+    onward(2, 1)
     unit(1, 1)
     unit(3, 1)
+    relay(0, 1)
+    relay(0, 2)
     relay(2, 0)
-    relay(0, 1)
+    for r in (0, 1, 3, 2):
+        finish(r, 0)
     relay(1, 1)
     relay(3, 1)
-    for r in (0, 1, 3, 2):
-        finish(r, 0)
-    far[2].wait_recv()
-    far[3].wait_recv()
+    came_far(1)
     unit(2, 1)
+    relay(1, 2)
+    relay(3, 2)
+    came_far(2)
+    unit(2, 2)
     relay(2, 1)
     for r in (0, 1, 3, 2):
         finish(r, 1)
+    relay(2, 2)
+    for r in (0, 1, 3, 2):
+        finish(r, 2)
     for copy in kept:
         copy.wait()
     for r in range(RING):
@@ -430,9 +456,11 @@
             pltpu.VMEM((RING * total, width // RING), BF16),
             dma((hidden_units // 128 * 2 + 3,)),
         ]
-        + [dma((RING,))] * 10
-        + [dma((RING, 2, RING))] * 2
-        + [dma((RING, 2, 2))] * 2
+        + [dma((RING,))] * 6
+        + [dma((3, 2))] * 2
+        + [dma((RING,))] * 2
+        + [dma((RING, 3, RING))] * 2
+        + [dma((RING, 3, 2))] * 2
         + [dma((RING, RING))] * 2,
         compiler_params=pltpu.CompilerParams(
             collective_id=1, has_side_effects=True, vmem_limit_bytes=VMEM_BYTES
@@ -461,7 +489,7 @@
         for d in range(RING):
             slot = meta[pl.ds(r * 2 * RING + d, 1)]
             gate = meta[pl.ds(r * 2 * RING + RING + d, 1)]
-            matrix[pl.ds((r * RING + d) * slots, slots)] = jnp.where(slot == place, gate, 0.0).astype(BF16)
+            matrix[pl.ds((r * RING + PLACE[d]) * slots, slots)] = jnp.where(slot == place, gate, 0.0).astype(BF16)
 
     def term(block):
         span = pl.ds(pl.multiple_of(group_of(block) * RING * slots, RING * slots), RING * slots)
@@ -472,11 +500,18 @@
             preferred_element_type=F32,
         )
 
-    share_out[...] = sum_over_tp(term, scratch).astype(BF16)
-    copy = remote(share_out, share_in, share_send.at[0], share_recv.at[0], target)
-    copy.start()
-    copy.wait()
-    layer_out[...] = (share_in[...].astype(F32) + state[...].astype(F32)).astype(BF16)
+    shares = []
+
+    def give(h, span, total):
+        share_out[span] = total.astype(BF16)
+        copy = remote(share_out.at[span], share_in.at[span], share_send.at[h], share_recv.at[h], target)
+        copy.start()
+        shares.append((span, copy))
+
+    sum_over_tp(term, give, scratch)
+    for span, copy in shares:
+        copy.wait()
+        layer_out[span] = (share_in[span].astype(F32) + state[span].astype(F32)).astype(BF16)
 
 
 def mix(meta, back, state):
@@ -490,8 +525,8 @@
             pltpu.VMEM((rows, width), BF16),
             pltpu.VMEM((rows, width), BF16),
             pltpu.VMEM((back.shape[0], rows), BF16),
-            pltpu.SemaphoreType.DMA((1,)),
-            pltpu.SemaphoreType.DMA((1,)),
+            pltpu.SemaphoreType.DMA((2,)),
+            pltpu.SemaphoreType.DMA((2,)),
         ]
         + sum_scratch(rows, width),
         compiler_params=pltpu.CompilerParams(

time: 237 us -> 216 us (0.911)
  Pallas kernels: 220 us -> 201 us
    pallas_call x1, Pallas kernels: 138 us -> 126 us  [experts(): pl.pallas_call(experts_kernel, out_shape=(jax.ShapeDtypeStruct((RING * to...]
    pallas_call x1, Pallas kernels: 48.7 us -> 44.6 us  [attend(): pl.pallas_call(attend_kernel, out_shape=(jax.ShapeDtypeStruct((rows, mode...]
    pallas_call x1, Pallas kernels: 33.7 us -> 30 us  [mix(): pl.pallas_call(mix_kernel, out_shape=jax.ShapeDtypeStruct((rows, width),...]
where the time goes in v3:
time: 216 us; the launch traced here: 214 us
  Pallas kernels  201 us (93%)
  other arithmetic  5.56 us (3%)
  matrix products  4.87 us (2%)
  local copies, waits for them, and re-layouts  2.33 us (1%)
    pallas_call x1, Pallas kernels, experts(): pl.pallas_call(experts_kernel, out_shape=(jax.ShapeDtypeStruct((RING * to...  126 us
    pallas_call x1, Pallas kernels, attend(): pl.pallas_call(attend_kernel, out_shape=(jax.ShapeDtypeStruct((rows, mode...  44.6 us
    pallas_call x1, Pallas kernels, mix(): pl.pallas_call(mix_kernel, out_shape=jax.ShapeDtypeStruct((rows, width),...  30 us

profile of v3, /device:TPU:32, one launch (start us, length us, event | category | flops | bytes accessed | tf_op | source)
XLA Modules:
  0.0 213.8 jit_solution(16770613600458075730)
XLA Ops:
  0.0 0.0 copy-start
  0.0 0.1 iota_compare_fusion.3
  0.1 0.8 compare_reduce_fusion
  0.9 0.1 eq.72
  1.0 0.2 select_convert_fusion
  1.2 0.8 fusion.7
  2.0 0.7 convert_element_type.23
  2.7 0.1 fusion.8
  2.8 44.6 %attend.1 = (bf16[256,4096]{1,0:T(8,128)(2,1)}, bf16[1536,1024]{1,0:T(8,128)(2,1)}) custom-call(bf16[256,256]{1,0:T(8,128)(2,1)} %context.1, bf16[256,4096]{1,0:T(8,128)(2,1)} %weight.1, bf16[256,256]{1,0:T(8,128)(2,1)} %residual.1, bf16[384,4096]{1,0:T(8,128)(2,1)} %bitcast.14), custom_call_target="tpu_custom_call" | custom-call | tf_op jit(solution)/shard_map/attend/pallas_call | solution.py:210
  47.4 0.0 copy-start.1
  47.4 2.2 %fusion = f32[256]{0:T(256)S(1)} fusion(bf16[256,4096]{1,0:T(8,128)(2,1)} %get-tuple-element.9), kind=kLoop, calls=%fused_computation.3 | loop fusion | flops 3145472 | bytes 2098176 | tf_op jit(solution)/shard_map/reduce_sum | solution.py:545
  49.6 0.0 copy-done
  49.6 2.4 %select_reduce_fusion.1 = (f32[256]{0:T(256)S(1)}, f32[256,64]{0,1:T(8,128)S(1)}) fusion(pred[256,64]{0,1:T(8,128)(4,1)S(1)} %fusion.7, bf16[64,4096]{1,0:T(8,128)(2,1)S(1)} %copy-done, bf16[256,4096]{1,0:T(8,128)(2,1)} %get-tuple-element.9, f32[4096]{0:T(1024)S(1)} %convert_element_type.23, f32[256]{0:T(256)S(1)} %add_rsqrt_fusion), kind=kOutput, calls=%fused_computation.16 | convolution fusion | flops 138444544 | bytes 2721792 | tf_op jit(solution)/shard_map/dot_general | solution.py:547
  52.1 0.1 select_reduce_fusion
  52.3 0.6 maximum_bitcast_fusion.meta
  52.9 0.0 copy-done.1
  52.9 0.7 constant_dynamic-slice_fusion.state
  53.5 2.3 %convolution_convert_fusion.packed = bf16[256,4096]{1,0:T(8,128)(2,1)} fusion(pred[256,256]{0,1:T(32,128)(4,1)S(1)} %fusion.8, bf16[256,4096]{1,0:T(8,128)(2,1)S(1)} %copy-done.1, f32[4096]{0:T(1024)S(1)} %convert_element_type.23, f32[256]{0:T(256)S(1)} %add_rsqrt_fusion), kind=kOutput, calls=%fused_computation.2 | convolution fusion | flops 542113792 | bytes 4277248 | tf_op jit(solution)/shard_map/dot_general | solution.py:567
  55.8 126.3 %experts.1 = (bf16[1024,1024]{1,0:T(8,128)(2,1)}, f32[32,256]{1,0:T(8,128)}) custom-call(bf16[256,4096]{1,0:T(8,128)(2,1)} %convolution_convert_fusion.packed, f32[8,256]{1,0:T(8,128)} %maximum_bitcast_fusion.meta, bf16[4096,384]{1,0:T(8,128)(2,1)} %bitcast.15, bf16[4096,384]{1,0:T(8,128)(2,1)} %bitcast.16, bf16[1536,1024]{1,0:T(8,128)(2,1)} %get-tuple-element.10.down), custom_call_target="tpu_custom_call" | custom-call | tf_op jit(solution)/shard_map/experts/pallas_call | solution.py:443
  182.2 30.0 %mix.1 = bf16[256,256]{1,0:T(8,128)(2,1)} custom-call(f32[32,256]{1,0:T(8,128)} %get-tuple-element.11.meta, bf16[1024,1024]{1,0:T(8,128)(2,1)} %get-tuple-element.12.back, bf16[256,256]{1,0:T(8,128)(2,1)} %constant_dynamic-slice_fusion.state), custom_call_target="tpu_custom_call" | custom-call | tf_op jit(solution)/shard_map/mix/pallas_call | solution.py:519
  212.2 1.6 copy.21
  (5 shorter events, 0.1 us)
Async XLA Ops:
  0.0 49.6 %copy-start = (bf16[64,4096]{1,0:T(8,128)(2,1)S(1)}, bf16[64,4096]{1,0:T(8,128)(2,1)}, u32[]{:S(2)}) copy-start(bf16[64,4096]{1,0:T(8,128)(2,1)} %param.13) | copy-start | bytes 1572868
  47.4 5.5 %copy-start.1 = (bf16[256,4096]{1,0:T(8,128)(2,1)S(1)}, bf16[256,4096]{1,0:T(8,128)(2,1)}, u32[]{:S(2)}) copy-start(bf16[256,4096]{1,0:T(8,128)(2,1)} %get-tuple-element.9) | copy-start | bytes 6291460

commit v4 on v3

--- a/solution.py
+++ b/solution.py
@@ -16,6 +16,8 @@
 VMEM_BYTES = 58 * 2**20
 PLACE = (3, 0, 2, 1)
 STAGES = ((1, 3), (2,), (0,))
+ORDER = (0, 1, 7, 2, 6, 3, 5, 4)
+GROUPS = ((0, 1, 2), (3, 4), (5, 6, 7))
 DISTANCES = (4, 3, 5, 2, 6, 1, 7, 0)
 
 
@@ -120,129 +122,94 @@
         copy.wait_send()
 
 
-def gather_over_tp(out, width, sems):
-    arm_send, arm_recv, near_send, near_recv = sems
-    z, core, chips, partner, right, left = tp_place()
-    half = out.shape[0] // 2
-    copies = []
-
-    def at(j, h, side):
-        return out.at[pl.ds(h * half, half), columns(((z + j + chips) % chips) * 2 + side, width)]
-
-    def pass_on(arm, h, step):
-        ref = at(step if arm else -step, h, core)
-        copies.append(remote(ref, ref, arm_send.at[arm, step, h], arm_recv.at[arm, step, h], (right, left)[arm]))
-        copies[-1].start()
-
-    def to_partner(j, h):
-        ref = at(j, h, core)
-        copies.append(remote(ref, ref, near_send.at[j % 8, h], near_recv.at[j % 8, h], partner))
-        copies[-1].start()
-
-    def start(h):
+class GatherOverTp:
+    def __init__(self, out, width, sems):
+        self.out, self.width = out, width
+        self.arm_send, self.arm_recv, self.near_send, self.near_recv = sems
+        z, self.core, chips, self.partner, self.right, self.left = tp_place()
+        self.half = out.shape[0] // 2
+        self.copies = []
+
+    def at(self, j, h, side):
+        offset = pl.multiple_of((ORDER.index(j % 8) * 2 + side) * self.width, self.width)
+        return self.out.at[pl.ds(h * self.half, self.half), pl.ds(offset, self.width)]
+
+    def go(self, source, target, send, recv, device):
+        copy = remote(source, target, send, recv, device)
+        copy.start()
+        self.copies.append(copy)
+
+    def pass_on(self, arm, h, step):
+        sign = 1 if arm else -1
+        self.go(
+            self.at(sign * step, h, self.core),
+            self.at(sign * (step + 1), h, self.core),
+            self.arm_send.at[arm, step, h],
+            self.arm_recv.at[arm, step, h],
+            (self.right, self.left)[arm],
+        )
+
+    def to_partner(self, j, h):
+        ref = self.at(j, h, self.core)
+        self.go(ref, ref, self.near_send.at[j % 8, h], self.near_recv.at[j % 8, h], self.partner)
+
+    def start(self, h):
         for arm in (h, 1 - h):
-            pass_on(arm, h, 0)
-        to_partner(0, h)
-
-    def finish():
-        for step in range(1, 5):
-            for arm, h in ((0, 0), (1, 0), (1, 1), (0, 1)):
-                if step == 4 and arm != h:
-                    continue
-                j = step if arm else -step
-                ref = at(j, h, core)
-                remote(ref, ref, arm_send.at[arm, step - 1, h], arm_recv.at[arm, step - 1, h], right).wait_recv()
-                if step < 3 or (step == 3 and arm == h):
-                    pass_on(arm, h, step)
-                to_partner(j, h)
-        for j in range(8):
-            for h in range(2):
-                ref = at(j, h, 1 - core)
-                remote(ref, ref, near_send.at[j, h], near_recv.at[j, h], partner).wait_recv()
-        for copy in copies:
+            self.pass_on(arm, h, 0)
+        self.to_partner(0, h)
+
+    def step(self, step):
+        for arm, h in ((0, 0), (1, 0), (1, 1), (0, 1)):
+            if step == 4 and arm != h:
+                continue
+            j = step if arm else -step
+            ref = self.at(j, h, self.core)
+            remote(
+                ref, ref, self.arm_send.at[arm, step - 1, h], self.arm_recv.at[arm, step - 1, h], self.right
+            ).wait_recv()
+            if step < 3 or (step == 3 and arm == h):
+                self.pass_on(arm, h, step)
+            self.to_partner(j, h)
+
+    def ready(self, j):
+        for h in range(2):
+            ref = self.at(j, h, 1 - self.core)
+            remote(ref, ref, self.near_send.at[j % 8, h], self.near_recv.at[j % 8, h], self.partner).wait_recv()
+
+    def finish(self):
+        for copy in self.copies:
             copy.wait_send()
 
-    return start, finish
-
-
-def attend_kernel(context, weight, residual, down, hidden, spread, *scratch):
+
+def layer_kernel(
+    context, weight, residual, places, gain, router, ids, gate, up, down,
+    back, meta_all, state,
+    hidden, squares, selector, packed, meta, rows, gate_up, spread, inner, out, *scratch
+):
     total_scratch, gather_sems, (spread_send, spread_recv) = scratch[:9], scratch[9:13], scratch[13:15]
-    width = residual.shape[1]
+    (load, y_send, y_recv, right_send, right_recv, left_send, left_recv, far_send, far_recv, meta_send, meta_recv,
+     in_send, in_recv, on_send, on_recv, out_send, out_recv) = scratch[15:]
     tp, ep = lax.axis_index("tp"), lax.axis_index("ep")
     y, x = ep // RING, ep % RING
-    others = [(tp, y * RING + (x + k) % RING) for k in range(1, RING)]
-    z, core, chips, partner, right, left = tp_place()
-    greet([partner, right, left] + others)
-    depth, quarter = down.shape[0], down.shape[1] // RING
-    copies = []
-    for k in range(1, RING):
-        copy = remote(
-            down.at[:, columns((x + k) % RING, quarter)],
-            spread.at[pl.ds(k * depth, depth)],
-            spread_send.at[k],
-            spread_recv.at[k],
-            others[k - 1],
-        )
-        copy.start()
-        copies.append(copy)
-    keep = pltpu.make_async_copy(down.at[:, columns(x, quarter)], spread.at[pl.ds(0, depth)], spread_send.at[0])
-    keep.start()
-
-    def term(block):
-        return jnp.dot(context[...], weight[:, columns(block, width)], preferred_element_type=F32)
-
-    start, finish = gather_over_tp(hidden, width, gather_sems)
-
-    def give(h, span, total):
-        hidden[span, columns(tp, width)] = (total + residual[span].astype(F32)).astype(BF16)
-        start(h)
-
-    sum_over_tp(term, give, total_scratch)
-    finish()
-    keep.wait()
-    for copy in copies:
-        copy.wait()
-
-
-def attend(context, weight, residual, down):
-    rows, width = residual.shape
-    depth, model_width = down.shape
-    return pl.pallas_call(
-        attend_kernel,
-        out_shape=(
-            jax.ShapeDtypeStruct((rows, model_width), BF16),
-            jax.ShapeDtypeStruct((RING * depth, model_width // RING), BF16),
-        ),
-        in_specs=in_vmem(3) + [pl.BlockSpec(memory_space=pl.ANY)],
-        out_specs=(pl.BlockSpec(memory_space=pltpu.VMEM), pl.BlockSpec(memory_space=pl.ANY)),
-        scratch_shapes=sum_scratch(rows, width)
-        + [pltpu.SemaphoreType.DMA((2, 4, 2))] * 2
-        + [pltpu.SemaphoreType.DMA((8, 2))] * 2
-        + [pltpu.SemaphoreType.DMA((4,))] * 2,
-        compiler_params=pltpu.CompilerParams(
-            collective_id=0, has_side_effects=True, vmem_limit_bytes=VMEM_BYTES
-        ),
-        name="attend",
-    )(context, weight, residual, down)
-
-
-def experts_kernel(packed, meta, gate, up, down, back, meta_all, rows, gate_up, spread, inner, out, *sems):
-    (load, y_send, y_recv, right_send, right_recv, left_send, left_recv, far_send, far_recv, meta_send, meta_recv,
-     in_send, in_recv, on_send, on_recv, out_send, out_recv) = sems
-    tp, ep = lax.axis_index("tp"), lax.axis_index("ep")
-    y, x = ep // RING, ep % RING
-    slots = packed.shape[0] // RING
-    width = packed.shape[1]
+    z, core, chips, partner, z_right, z_left = tp_place()
+    tokens, share = residual.shape
+    slots = back.shape[0] // RING // RING
+    width = weight.shape[1]
     block = RING * slots
     hidden_units = gate.shape[1]
     pieces = hidden_units // 128
     quarter = width // RING
+    pair = 2 * share
 
     def device(dy, dx):
         return (tp, ((y + dy + RING) % RING) * RING + (x + dx + RING) % RING)
 
     right, left = device(0, 1), device(0, -1)
-    greet([device(0, k) for k in range(1, RING)] + [device(k, 0) for k in range(1, RING)])
+    greet(
+        [partner, z_right, z_left]
+        + [device(0, k) for k in range(1, RING)]
+        + [device(k, 0) for k in range(1, RING)]
+    )
 
     def chunk(r, d):
         return pl.ds(r * block + PLACE[d] * slots, slots)
@@ -265,41 +232,95 @@
         copies.append(copy)
         return copy
 
-    y_copies = {}
-    for d in (1, 3, 2):
-        y_copies[d] = send(packed.at[pl.ds(d * slots, slots)], rows.at[chunk(0, d)], y_send.at[d], y_recv.at[d], device(d, 0))
-
-    def to_sides(d, source):
-        return (
-            send(source, rows.at[chunk(1, d)], right_send.at[d], right_recv.at[d], right),
-            send(source, rows.at[chunk(3, d)], left_send.at[d], left_recv.at[d], left),
+    spreads = [
+        send(
+            down.at[:, columns((x + k) % RING, quarter)],
+            spread.at[pl.ds(k * hidden_units, hidden_units)],
+            spread_send.at[k],
+            spread_recv.at[k],
+            device(0, k),
         )
-
-    sides = {0: to_sides(0, packed.at[pl.ds(0, slots)])}
-    loads = []
-    for j in range(pieces):
-        loads.append((gate.at[:, pl.ds(j * 128, 128)], gate_up.at[:, pl.ds(j * 256, 128)]))
-        loads.append((up.at[:, pl.ds(j * 128, 128)], gate_up.at[:, pl.ds(j * 256 + 128, 128)]))
-    loads.append((down, spread))
-    loads.append((packed.at[pl.ds(0, slots)], rows.at[chunk(0, 0)]))
-    loads.append((meta, meta_all.at[pl.ds(0, 2 * RING)]))
+        for k in range(1, RING)
+    ]
+    loads = [(down.at[:, columns(x, quarter)], spread.at[pl.ds(0, hidden_units)])]
+    for p, j in enumerate(ORDER):
+        source = pl.ds(pl.multiple_of((z + j) % chips * pair, pair), pair)
+        target = pl.ds(p * pair, pair)
+        for i in range(pieces):
+            part = pl.ds(i * 128, 128)
+            loads.append((gate.at[source, part], gate_up.at[target, pl.ds(i * 256, 128)]))
+            loads.append((up.at[source, part], gate_up.at[target, pl.ds(i * 256 + 128, 128)]))
     loads = [pltpu.make_async_copy(a, b, load.at[i]) for i, (a, b) in enumerate(loads)]
     for copy in loads:
         copy.start()
-    metas = [
-        send(meta, meta_all.at[pl.ds(k * 2 * RING, 2 * RING)], meta_send.at[k], meta_recv.at[k], device(0, k))
-        for k in range(1, RING)
-    ]
-
-    def y_arrived(d):
-        y_copies[d].wait_recv()
-        sides[d] = to_sides(d, rows.at[chunk(0, d)])
+    place = lax.broadcasted_iota(jnp.int32, (slots, tokens), 0).astype(F32)
+    for d in range(RING):
+        selector[pl.ds(PLACE[d] * slots, slots)] = jnp.where(places[pl.ds(d, 1)] == place, 1.0, 0.0).astype(BF16)
+    squares[...] = jnp.zeros_like(squares)
+    gather = GatherOverTp(hidden, share, gather_sems)
+
+    def term(index):
+        return jnp.dot(context[...], weight[:, columns(index, share)], preferred_element_type=F32)
+
+    def give(h, span, total):
+        mine = (total + residual[span].astype(F32)).astype(BF16)
+        state[span] = mine
+        hidden[span, columns(core, share)] = mine
+        gather.start(h)
+
+    sum_over_tp(term, give, total_scratch)
+    y_copies, sides = {}, {}
+
+    def group_columns(g):
+        first, last = GROUPS[g][0], GROUPS[g][-1] + 1
+        return pl.ds(first * pair, (last - first) * pair + (128 if g == len(GROUPS) - 1 else 0))
+
+    def to_sides(d, g, source):
+        part = group_columns(g)
+        sides[d, g] = (
+            send(source, rows.at[chunk(1, d), part], right_send.at[d, g], right_recv.at[d, g], right),
+            send(source, rows.at[chunk(3, d), part], left_send.at[d, g], left_recv.at[d, g], left),
+        )
+
+    def y_arrived(d, g):
+        y_copies[d, g].wait_recv()
+        to_sides(d, g, rows.at[chunk(0, d), group_columns(g)])
+
+    def dispatch(g):
+        for p in GROUPS[g]:
+            gather.ready(ORDER[p])
+            part = pl.ds(p * pair, pair)
+            value = hidden[:, part].astype(F32)
+            total = squares[...]
+            for i in range(pair // 128):
+                lanes = value[:, i * 128 : (i + 1) * 128]
+                total = total + lanes * lanes
+            squares[...] = total
+            scaled = (value * gain[:, columns((z + ORDER[p]) % chips, pair)]).astype(BF16)
+            packed[:, part] = jnp.dot(selector[...], scaled, preferred_element_type=F32).astype(BF16)
+        if g == len(GROUPS) - 1:
+            mean = jnp.sum(squares[...], axis=1, keepdims=True) / width
+            inverse = lax.rsqrt(mean + epsilon)
+            high = inverse.astype(BF16).astype(F32)
+            lane = lax.broadcasted_iota(jnp.int32, (tokens, 128), 1)
+            parts = jnp.where(lane == 0, high, jnp.where(lane == 1, inverse - high, 0.0)).astype(BF16)
+            packed[:, pl.ds(width, 128)] = jnp.dot(selector[...], parts, preferred_element_type=F32).astype(BF16)
+        part = group_columns(g)
+        for d in (1, 3, 2):
+            y_copies[d, g] = send(
+                packed.at[chunk(0, d), part], rows.at[chunk(0, d), part], y_send.at[d, g], y_recv.at[d, g], device(d, 0)
+            )
+        to_sides(0, g, packed.at[chunk(0, 0), part])
+        rows[chunk(0, 0), part] = packed[chunk(0, 0), part]
 
     def unit(r, h):
         span = unit_span(r, h)
+        parts = rows[span, pl.ds(width, 128)].astype(F32)
+        inverse = parts[:, 0:1] + parts[:, 1:2]
 
         def step(j, carry):
-            both = jnp.dot(rows[span], gate_up[:, columns(j, 256)], preferred_element_type=F32)
+            both = jnp.dot(rows[span, pl.ds(0, width)], gate_up[:, columns(j, 256)], preferred_element_type=F32)
+            both = both * inverse
             value, scale = both[:, :128], both[:, 128:]
             inner[span, columns(j, 128)] = (value / (1.0 + jnp.exp(-value)) * scale).astype(BF16)
             return carry
@@ -329,10 +350,12 @@
             )
 
     def came_right(d):
-        sides[d][0].wait_recv()
+        for g in range(len(GROUPS)):
+            sides[d, g][0].wait_recv()
 
     def came_left(d):
-        sides[d][1].wait_recv()
+        for g in range(len(GROUPS)):
+            sides[d, g][1].wait_recv()
 
     far = {}
 
@@ -371,16 +394,59 @@
             else:
                 send(out.at[chunk(r, d)], target, out_send.at[r, d], out_recv.at[r, d], device(-d, 0))
 
-    kept = []
-    y_arrived(1)
-    y_arrived(3)
+    def gates():
+        inverse = lax.rsqrt(jnp.sum(squares[...], axis=1, keepdims=True) / width + epsilon)
+        count = router.shape[0]
+        logits = jnp.zeros((tokens, count), F32)
+        for p, j in enumerate(ORDER):
+            part = columns((z + j) % chips, pair)
+            normed = (hidden[:, pl.ds(p * pair, pair)].astype(F32) * inverse * gain[:, part]).astype(BF16)
+            logits = logits + lax.dot_general(
+                normed, router[:, part], (((1,), (1,)), ((), ())), preferred_element_type=F32
+            )
+        every = lax.broadcasted_iota(jnp.int32, (tokens, count), 1)
+        hit = every == ids[:, 0:1]
+        for k in range(1, ids.shape[1]):
+            hit = hit | (every == ids[:, k : k + 1])
+        top = jnp.max(jnp.where(hit, logits, -jnp.inf), axis=1, keepdims=True)
+        raised = jnp.where(hit, jnp.exp(jnp.where(hit, logits - top, 0.0)), 0.0)
+        softmax = raised / jnp.sum(raised, axis=1, keepdims=True)
+        lane = lax.broadcasted_iota(jnp.int32, (tokens, 128), 1)
+        own = jnp.zeros((tokens, 128), F32)
+        for d in range(RING):
+            value = jnp.sum(jnp.where(every == tp * RING + (y + d) % RING, softmax, 0.0), axis=1, keepdims=True)
+            own = own + jnp.where(lane == d, value, 0.0)
+        meta[pl.ds(0, RING)] = places[pl.ds(0, RING)]
+        meta[pl.ds(RING, RING)] = own.T[:RING]
+
+    gather.step(1)
+    dispatch(0)
+    gather.step(2)
+    dispatch(1)
+    y_arrived(1, 0)
+    y_arrived(3, 0)
+    gather.step(3)
+    gather.step(4)
+    dispatch(2)
+    y_arrived(1, 1)
+    y_arrived(3, 1)
+    gates()
+    meta_all[pl.ds(0, 2 * RING)] = meta[...]
+    metas = [
+        send(meta, meta_all.at[pl.ds(k * 2 * RING, 2 * RING)], meta_send.at[k], meta_recv.at[k], device(0, k))
+        for k in range(1, RING)
+    ]
+    y_arrived(1, 2)
+    y_arrived(3, 2)
     for copy in loads:
         copy.wait()
+    kept = []
     unit(0, 0)
     came_right(0)
     came_left(0)
     unit(0, 2)
-    y_arrived(2)
+    for g in range(3):
+        y_arrived(2, g)
     came_right(1)
     onward(0, 0)
     came_left(3)
@@ -408,6 +474,8 @@
     relay(0, 1)
     relay(0, 2)
     relay(2, 0)
+    for copy in spreads:
+        copy.wait_recv()
     for r in (0, 1, 3, 2):
         finish(r, 0)
     relay(1, 1)
@@ -432,41 +500,53 @@
             remote(ref, ref, out_send.at[r, d], out_recv.at[r, d], device(d, 0)).wait_recv()
     for copy in metas:
         copy.wait_recv()
+    gather.finish()
     for copy in copies:
         copy.wait_send()
 
 
-def experts(packed, meta, gate, up, down):
-    total, width = packed.shape
-    hidden_units = gate.shape[1]
+def layer(context, weight, residual, places, gain, router, ids, gate, up, down, slots):
+    tokens, share = residual.shape
+    width, hidden_units = gate.shape
+    total = RING * slots
     dma = pltpu.SemaphoreType.DMA
     return pl.pallas_call(
-        experts_kernel,
+        layer_kernel,
         out_shape=(
             jax.ShapeDtypeStruct((RING * total, width // RING), BF16),
-            jax.ShapeDtypeStruct((RING * meta.shape[0], meta.shape[1]), F32),
+            jax.ShapeDtypeStruct((RING * 2 * RING, tokens), F32),
+            jax.ShapeDtypeStruct((tokens, share), BF16),
         ),
-        in_specs=in_vmem(2) + [pl.BlockSpec(memory_space=pl.ANY)] * 3,
-        out_specs=tuple(in_vmem(2)),
+        in_specs=in_vmem(7) + [pl.BlockSpec(memory_space=pl.ANY)] * 3,
+        out_specs=tuple(in_vmem(3)),
         scratch_shapes=[
-            pltpu.VMEM((RING * total, width), BF16),
+            pltpu.VMEM((tokens, width), BF16),
+            pltpu.VMEM((tokens, 128), F32),
+            pltpu.VMEM((total, tokens), BF16),
+            pltpu.VMEM((total, width + 128), BF16),
+            pltpu.VMEM((2 * RING, tokens), F32),
+            pltpu.VMEM((RING * total, width + 128), BF16),
             pltpu.VMEM((width, 2 * hidden_units), BF16),
             pltpu.VMEM((RING * hidden_units, width // RING), BF16),
             pltpu.VMEM((RING * total, RING * hidden_units), BF16),
             pltpu.VMEM((RING * total, width // RING), BF16),
-            dma((hidden_units // 128 * 2 + 3,)),
         ]
-        + [dma((RING,))] * 6
+        + sum_scratch(tokens, share)
+        + [dma((2, 4, 2))] * 2
+        + [dma((8, 2))] * 2
+        + [dma((RING,))] * 2
+        + [dma((hidden_units // 128 * 16 + 1,))]
+        + [dma((RING, 3))] * 6
         + [dma((3, 2))] * 2
         + [dma((RING,))] * 2
         + [dma((RING, 3, RING))] * 2
         + [dma((RING, 3, 2))] * 2
         + [dma((RING, RING))] * 2,
         compiler_params=pltpu.CompilerParams(
-            collective_id=1, has_side_effects=True, vmem_limit_bytes=VMEM_BYTES
+            collective_id=0, has_side_effects=True, vmem_limit_bytes=VMEM_BYTES
         ),
-        name="experts",
-    )(packed, meta, gate, up, down)
+        name="layer",
+    )(context, weight, residual, places, gain, router, ids, gate, up, down)
 
 
 def mix_kernel(meta, back, state, layer_out, share_out, share_in, matrix, share_send, share_recv, *scratch):
@@ -530,56 +610,43 @@
         ]
         + sum_scratch(rows, width),
         compiler_params=pltpu.CompilerParams(
-            collective_id=2, has_side_effects=True, vmem_limit_bytes=VMEM_BYTES
+            collective_id=1, has_side_effects=True, vmem_limit_bytes=VMEM_BYTES
         ),
         name="mix",
     )(meta, back, state)
 
 
-def route(hidden, norm_gain, router_weight, expert_ids, capacity):
+def slots_of(expert_ids):
     tp, ep = lax.axis_index("tp"), lax.axis_index("ep")
-    y = ep // RING
-    rows = hidden.shape[0]
-    expert_count = router_weight.shape[0]
-    state_float = hidden.astype(F32)
-    inv_rms = lax.rsqrt(jnp.mean(state_float * state_float, axis=1, keepdims=True) + epsilon)
-    normed = (state_float * inv_rms * norm_gain.astype(F32)).astype(BF16)
-    logits = lax.dot_general(normed, router_weight, (((1,), (1,)), ((), ())), preferred_element_type=F32)
-    every = lax.broadcasted_iota(jnp.int32, (1, 1, expert_count), 2)
-    hit_all = jnp.any(expert_ids[:, :, None] == every, axis=1)
-    top = jnp.max(jnp.where(hit_all, logits, -jnp.inf), axis=1, keepdims=True)
-    raised = jnp.where(hit_all, jnp.exp(jnp.where(hit_all, logits - top, 0.0)), 0.0)
-    gates_all = raised / jnp.sum(raised, axis=1, keepdims=True)
-    mine = tp * RING + (y + lax.broadcasted_iota(jnp.int32, (1, 1, RING), 2)) % RING
-    hit = jnp.any(expert_ids[:, :, None] == mine, axis=1)
-    own_gates = jnp.sum(
-        jnp.where(lax.broadcasted_iota(jnp.int32, (1, expert_count, 1), 1) == mine, gates_all[:, :, None], 0.0), axis=1
-    )
-    before = (
-        lax.broadcasted_iota(jnp.int32, (rows, rows), 1) <= lax.broadcasted_iota(jnp.int32, (rows, rows), 0)
+    rows = expert_ids.shape[0]
+    mine = tp * RING + (ep // RING + lax.broadcasted_iota(jnp.int32, (1, RING, 1), 1)) % RING
+    hit = jnp.any(expert_ids.T[:, None, :] == mine.reshape(1, RING, 1), axis=0)
+    upto = (
+        lax.broadcasted_iota(jnp.int32, (rows, rows), 0) <= lax.broadcasted_iota(jnp.int32, (rows, rows), 1)
     ).astype(BF16)
-    slot_of = jnp.dot(before, hit.astype(BF16), preferred_element_type=F32).astype(jnp.int32) - 1
-    slots = lax.broadcasted_iota(jnp.int32, (1, 1, capacity), 2)
-    chosen = (slot_of[:, :, None] == slots) & hit[:, :, None]
-    selector = chosen.astype(BF16).reshape(rows, RING * capacity)
-    places = jnp.where(hit, slot_of, -1).astype(F32)
-    meta = jnp.concatenate([places, own_gates], axis=1).T
-    packed = lax.dot_general(
-        selector, normed, (((0,), (0,)), ((), ())), preferred_element_type=F32
-    ).astype(BF16)
-    return packed, meta
+    count = jnp.dot(hit.astype(BF16), upto, preferred_element_type=F32)
+    places = jnp.where(hit, count - 1.0, -1.0)
+    return jnp.concatenate([places, places], axis=0)
 
 
 def shards(
     context, out_weight, residual, norm_gain, router_weight, expert_ids, w_gate, w_up, w_down
 ):
-    tp = lax.axis_index("tp")
-    rows, width = residual.shape
-    hidden, spread_down = attend(context, out_weight, residual, w_down[0])
+    rows = residual.shape[0]
     capacity = min(rows, 2 * rows * expert_ids.shape[1] // router_weight.shape[0])
-    packed, meta = route(hidden, norm_gain, router_weight, expert_ids, capacity)
-    back, meta_all = experts(packed, meta, w_gate[0], w_up[0], spread_down)
-    state = lax.dynamic_slice_in_dim(hidden, tp * width, width, 1)
+    back, meta_all, state = layer(
+        context,
+        out_weight,
+        residual,
+        slots_of(expert_ids),
+        norm_gain.astype(F32)[None],
+        router_weight,
+        expert_ids,
+        w_gate[0],
+        w_up[0],
+        w_down[0],
+        capacity,
+    )
     return mix(meta_all, back, state)
 
 

time: 216 us -> 206 us (0.954)
  matrix products: 4.87 us -> 0.15 us
  Pallas kernels: 201 us -> 197 us
  other arithmetic: 5.56 us -> 2.71 us
    pallas_call x2 -> x1, Pallas kernels: 171 us -> 165 us  [layer(): pl.pallas_call(layer_kernel, out_shape=(jax.ShapeDtypeStruct((RING * tota...]
    dot_general x3 -> x1, matrix products: 4.87 us -> 0.15 us  [slots_of(): count = jnp.dot(hit.astype(BF16), upto, preferred_element_type=F32)]
    pallas_call x1, Pallas kernels: 30 us -> 32.8 us  [mix(): pl.pallas_call(mix_kernel, out_shape=jax.ShapeDtypeStruct((rows, width),...]
    reduce_sum x3 -> x0, other arithmetic: 2.39 us -> none  [the longest x1 2.23 us: route(): jnp.mean(state_float * state_float, axis=1, keepdims=True) + epsilon]
where the time goes in v4:
time: 206 us; the launch traced here: 203 us
  Pallas kernels  197 us (96%)
  local copies, waits for them, and re-layouts  3.05 us (1%)
  other arithmetic  2.71 us (1%)
    pallas_call x1, Pallas kernels, layer(): pl.pallas_call(layer_kernel, out_shape=(jax.ShapeDtypeStruct((RING * tota...  165 us
    pallas_call x1, Pallas kernels, mix(): pl.pallas_call(mix_kernel, out_shape=jax.ShapeDtypeStruct((rows, width),...  32.8 us

profile of v4, /device:TPU:32, one launch (start us, length us, event | category | flops | bytes accessed | tf_op | source)
XLA Modules:
  0.0 203.3 jit_solution(11681266589576067890)
XLA Ops:
  0.0 0.8 compare_reduce_fusion
  0.8 0.1 fusion
  0.9 0.6 pad_maximum_fusion.places
  1.6 1.3 broadcast_in_dim.10
  2.9 1.5 copy.11.ids
  4.3 164.5 %layer.1 = (bf16[1024,1024]{1,0:T(8,128)(2,1)}, f32[32,256]{1,0:T(8,128)}, bf16[256,256]{1,0:T(8,128)(2,1)}) custom-call(bf16[256,256]{1,0:T(8,128)(2,1)} %context.1, bf16[256,4096]{1,0:T(8,128)(2,1)} %weight.1, bf16[256,256]{1,0:T(8,128)(2,1)} %residual.1, f32[8,256]{1,0:T(8,128)} %pad_maximum_fusion.places, f32[1,4096]{1,0:T(1,128)} %bitcast.9, ...), custom_call_target="tpu_custom_call" | custom-call | tf_op jit(solution)/shard_map/layer/pallas_call | solution.py:513
  168.9 32.8 %mix.1 = bf16[256,256]{1,0:T(8,128)(2,1)} custom-call(f32[32,256]{1,0:T(8,128)} %get-tuple-element.8.meta, bf16[1024,1024]{1,0:T(8,128)(2,1)} %get-tuple-element.9.back, bf16[256,256]{1,0:T(8,128)(2,1)} %get-tuple-element.10.state), custom_call_target="tpu_custom_call" | custom-call | tf_op jit(solution)/shard_map/mix/pallas_call | solution.py:599
  201.7 1.6 copy.13
  (1 shorter events, 0.0 us)

commit v5 on v4

--- a/solution.py
+++ b/solution.py
@@ -184,11 +184,12 @@
 def layer_kernel(
     context, weight, residual, places, gain, router, ids, gate, up, down,
     back, meta_all, state,
-    hidden, squares, selector, packed, meta, rows, gate_up, spread, inner, out, *scratch
+    hidden, dense, squares, places_all, selector, packed, packed_far, meta, rows, gate_up, spread, inner, out, *scratch
 ):
     total_scratch, gather_sems, (spread_send, spread_recv) = scratch[:9], scratch[9:13], scratch[13:15]
     (load, y_send, y_recv, right_send, right_recv, left_send, left_recv, far_send, far_recv, meta_send, meta_recv,
-     in_send, in_recv, on_send, on_recv, out_send, out_recv) = scratch[15:]
+     in_send, in_recv, on_send, on_recv, out_send, out_recv,
+     place_send, place_recv, dense_send, dense_recv, beyond_send, beyond_recv) = scratch[15:]
     tp, ep = lax.axis_index("tp"), lax.axis_index("ep")
     y, x = ep // RING, ep % RING
     z, core, chips, partner, z_right, z_left = tp_place()
@@ -200,6 +201,8 @@
     pieces = hidden_units // 128
     quarter = width // RING
     pair = 2 * share
+    early = GROUPS[2][0] * pair
+    late = pl.ds(early, width + 128 - early)
 
     def device(dy, dx):
         return (tp, ((y + dy + RING) % RING) * RING + (x + dx + RING) % RING)
@@ -240,6 +243,10 @@
             spread_recv.at[k],
             device(0, k),
         )
+        for k in range(1, RING)
+    ]
+    place_copies = [
+        send(places, places_all.at[pl.ds(k * 2 * RING, 2 * RING)], place_send.at[k], place_recv.at[k], device(0, k))
         for k in range(1, RING)
     ]
     loads = [(down.at[:, columns(x, quarter)], spread.at[pl.ds(0, hidden_units)])]
@@ -254,8 +261,13 @@
     for copy in loads:
         copy.start()
     place = lax.broadcasted_iota(jnp.int32, (slots, tokens), 0).astype(F32)
-    for d in range(RING):
-        selector[pl.ds(PLACE[d] * slots, slots)] = jnp.where(places[pl.ds(d, 1)] == place, 1.0, 0.0).astype(BF16)
+
+    def select(r, source, first):
+        for d in range(RING):
+            hit = source[pl.ds(first + d, 1)] == place
+            selector[pl.ds(r * block + PLACE[d] * slots, slots)] = jnp.where(hit, 1.0, 0.0).astype(BF16)
+
+    select(0, places, 0)
     squares[...] = jnp.zeros_like(squares)
     gather = GatherOverTp(hidden, share, gather_sems)
 
@@ -269,7 +281,7 @@
         gather.start(h)
 
     sum_over_tp(term, give, total_scratch)
-    y_copies, sides = {}, {}
+    y_copies, sides, denses, far_copies = {}, {}, {}, {}
 
     def group_columns(g):
         first, last = GROUPS[g][0], GROUPS[g][-1] + 1
@@ -284,7 +296,8 @@
 
     def y_arrived(d, g):
         y_copies[d, g].wait_recv()
-        to_sides(d, g, rows.at[chunk(0, d), group_columns(g)])
+        if g < 2:
+            to_sides(d, g, rows.at[chunk(0, d), group_columns(g)])
 
     def dispatch(g):
         for p in GROUPS[g]:
@@ -297,23 +310,63 @@
                 total = total + lanes * lanes
             squares[...] = total
             scaled = (value * gain[:, columns((z + ORDER[p]) % chips, pair)]).astype(BF16)
-            packed[:, part] = jnp.dot(selector[...], scaled, preferred_element_type=F32).astype(BF16)
+            packed[:, part] = jnp.dot(selector[pl.ds(0, block)], scaled, preferred_element_type=F32).astype(BF16)
         if g == len(GROUPS) - 1:
             mean = jnp.sum(squares[...], axis=1, keepdims=True) / width
             inverse = lax.rsqrt(mean + epsilon)
             high = inverse.astype(BF16).astype(F32)
             lane = lax.broadcasted_iota(jnp.int32, (tokens, 128), 1)
             parts = jnp.where(lane == 0, high, jnp.where(lane == 1, inverse - high, 0.0)).astype(BF16)
-            packed[:, pl.ds(width, 128)] = jnp.dot(selector[...], parts, preferred_element_type=F32).astype(BF16)
+            hidden[:, pl.ds(width, 128)] = parts
+            packed[:, pl.ds(width, 128)] = jnp.dot(
+                selector[pl.ds(0, block)], parts, preferred_element_type=F32
+            ).astype(BF16)
+            denses[1] = send(hidden.at[:, late], dense.at[pl.ds(0, tokens)], dense_send.at[1], dense_recv.at[1], right)
+            denses[3] = send(
+                hidden.at[:, late], dense.at[pl.ds(2 * tokens, tokens)], dense_send.at[3], dense_recv.at[3], left
+            )
         part = group_columns(g)
         for d in (1, 3, 2):
             y_copies[d, g] = send(
                 packed.at[chunk(0, d), part], rows.at[chunk(0, d), part], y_send.at[d, g], y_recv.at[d, g], device(d, 0)
             )
-        to_sides(0, g, packed.at[chunk(0, 0), part])
+        if g < 2:
+            to_sides(0, g, packed.at[chunk(0, 0), part])
         rows[chunk(0, 0), part] = packed[chunk(0, 0), part]
 
+    def dense_onward(side):
+        half = tokens // 2
+        r = (1, 3)[side]
+        denses[r].wait_recv()
+        denses[2, side] = send(
+            dense.at[pl.ds((r - 1) * tokens + side * half, half)],
+            dense.at[pl.ds(tokens + side * half, half)],
+            beyond_send.at[side],
+            beyond_recv.at[side],
+            (right, left)[side],
+        )
+
+    def pack_far(r):
+        place_copies[r - 1].wait_recv()
+        select(r, places_all, r * 2 * RING)
+        chosen = selector[pl.ds(r * block, block)]
+        span, target = pl.ds((r - 1) * tokens, tokens), pl.ds((r - 1) * block, block)
+        for p in GROUPS[2]:
+            part = pl.ds(p * pair - early, pair)
+            scaled = (dense[span, part].astype(F32) * gain[:, columns((z + ORDER[p]) % chips, pair)]).astype(BF16)
+            packed_far[target, part] = jnp.dot(chosen, scaled, preferred_element_type=F32).astype(BF16)
+        part = pl.ds(width - early, 128)
+        packed_far[target, part] = jnp.dot(chosen, dense[span, part], preferred_element_type=F32).astype(BF16)
+        for d in (1, 3, 2):
+            far_copies[r, d] = send(
+                packed_far.at[chunk(r - 1, d)], rows.at[chunk(r, d), late], y_send.at[d, r + 2], y_recv.at[d, r + 2], device(d, 0)
+            )
+        rows[chunk(r, 0), late] = packed_far[chunk(r - 1, 0)]
+
     def unit(r, h):
+        for d in STAGES[h]:
+            if r and d:
+                far_copies[r, d].wait_recv()
         span = unit_span(r, h)
         parts = rows[span, pl.ds(width, 128)].astype(F32)
         inverse = parts[:, 0:1] + parts[:, 1:2]
@@ -350,19 +403,19 @@
             )
 
     def came_right(d):
-        for g in range(len(GROUPS)):
+        for g in range(2):
             sides[d, g][0].wait_recv()
 
     def came_left(d):
-        for g in range(len(GROUPS)):
+        for g in range(2):
             sides[d, g][1].wait_recv()
 
     far = {}
 
     def onward(h, side):
         far[h, side] = send(
-            rows.at[half_span((1, 3)[side], h, side)],
-            rows.at[half_span(2, h, side)],
+            rows.at[half_span((1, 3)[side], h, side), pl.ds(0, early)],
+            rows.at[half_span(2, h, side), pl.ds(0, early)],
             far_send.at[h, side],
             far_recv.at[h, side],
             (right, left)[side],
@@ -442,17 +495,24 @@
         copy.wait()
     kept = []
     unit(0, 0)
-    came_right(0)
-    came_left(0)
     unit(0, 2)
     for g in range(3):
         y_arrived(2, g)
+    dense_onward(0)
+    dense_onward(1)
+    pack_far(1)
+    pack_far(3)
+    came_right(0)
+    came_left(0)
     came_right(1)
     onward(0, 0)
     came_left(3)
     onward(0, 1)
     came_left(1)
     came_right(3)
+    denses[2, 0].wait_recv()
+    denses[2, 1].wait_recv()
+    pack_far(2)
     unit(1, 0)
     unit(3, 0)
     relay(0, 0)
@@ -509,6 +569,7 @@
     tokens, share = residual.shape
     width, hidden_units = gate.shape
     total = RING * slots
+    late = width + 128 - GROUPS[2][0] * 2 * share
     dma = pltpu.SemaphoreType.DMA
     return pl.pallas_call(
         layer_kernel,
@@ -520,10 +581,13 @@
         in_specs=in_vmem(7) + [pl.BlockSpec(memory_space=pl.ANY)] * 3,
         out_specs=tuple(in_vmem(3)),
         scratch_shapes=[
-            pltpu.VMEM((tokens, width), BF16),
+            pltpu.VMEM((tokens, width + 128), BF16),
+            pltpu.VMEM((3 * tokens, late), BF16),
             pltpu.VMEM((tokens, 128), F32),
-            pltpu.VMEM((total, tokens), BF16),
+            pltpu.VMEM((RING * 2 * RING, tokens), F32),
+            pltpu.VMEM((RING * total, tokens), BF16),
             pltpu.VMEM((total, width + 128), BF16),
+            pltpu.VMEM((3 * total, late), BF16),
             pltpu.VMEM((2 * RING, tokens), F32),
             pltpu.VMEM((RING * total, width + 128), BF16),
             pltpu.VMEM((width, 2 * hidden_units), BF16),
@@ -536,12 +600,15 @@
         + [dma((8, 2))] * 2
         + [dma((RING,))] * 2
         + [dma((hidden_units // 128 * 16 + 1,))]
-        + [dma((RING, 3))] * 6
+        + [dma((RING, 6))] * 2
+        + [dma((RING, 3))] * 4
         + [dma((3, 2))] * 2
         + [dma((RING,))] * 2
         + [dma((RING, 3, RING))] * 2
         + [dma((RING, 3, 2))] * 2
-        + [dma((RING, RING))] * 2,
+        + [dma((RING, RING))] * 2
+        + [dma((RING,))] * 4
+        + [dma((2,))] * 2,
         compiler_params=pltpu.CompilerParams(
             collective_id=0, has_side_effects=True, vmem_limit_bytes=VMEM_BYTES
         ),

time: 206 us -> 207 us (level)
  no operation moved by 1% of the time
where the time goes in v5:
time: 207 us; the launch traced here: 204 us
  Pallas kernels  198 us (96%)
  local copies, waits for them, and re-layouts  3.05 us (1%)
  other arithmetic  2.71 us (1%)
    pallas_call x1, Pallas kernels, layer(): pl.pallas_call(layer_kernel, out_shape=(jax.ShapeDtypeStruct((RING * tota...  165 us
    pallas_call x1, Pallas kernels, mix(): pl.pallas_call(mix_kernel, out_shape=jax.ShapeDtypeStruct((rows, width),...  32.8 us

profile of v5, /device:TPU:32, one launch (start us, length us, event | category | flops | bytes accessed | tf_op | source)
XLA Modules:
  0.0 204.1 jit_solution(13818834663608482220)
XLA Ops:
  0.0 0.8 compare_reduce_fusion
  0.8 0.1 fusion
  0.9 0.6 pad_maximum_fusion.places
  1.6 1.3 broadcast_in_dim.10
  2.9 1.5 copy.11.ids
  4.3 165.3 %layer.1 = (bf16[1024,1024]{1,0:T(8,128)(2,1)}, f32[32,256]{1,0:T(8,128)}, bf16[256,256]{1,0:T(8,128)(2,1)}) custom-call(bf16[256,256]{1,0:T(8,128)(2,1)} %context.1, bf16[256,4096]{1,0:T(8,128)(2,1)} %weight.1, bf16[256,256]{1,0:T(8,128)(2,1)} %residual.1, f32[8,256]{1,0:T(8,128)} %pad_maximum_fusion.places, f32[1,4096]{1,0:T(1,128)} %bitcast.9, ...), custom_call_target="tpu_custom_call" | custom-call | tf_op jit(solution)/shard_map/layer/pallas_call | solution.py:574
  169.7 32.8 %mix.1 = bf16[256,256]{1,0:T(8,128)(2,1)} custom-call(f32[32,256]{1,0:T(8,128)} %get-tuple-element.8.meta, bf16[1024,1024]{1,0:T(8,128)(2,1)} %get-tuple-element.9.back, bf16[256,256]{1,0:T(8,128)(2,1)} %get-tuple-element.10.state), custom_call_target="tpu_custom_call" | custom-call | tf_op jit(solution)/shard_map/mix/pallas_call | solution.py:666
  202.5 1.6 copy.13
  (1 shorter events, 0.0 us)

commit v6 on v4

--- a/solution.py
+++ b/solution.py
@@ -183,17 +183,18 @@
 
 def layer_kernel(
     context, weight, residual, places, gain, router, ids, gate, up, down,
-    back, meta_all, state,
-    hidden, squares, selector, packed, meta, rows, gate_up, spread, inner, out, *scratch
+    share_in, state,
+    back, meta_all, matrix, share_out, hidden, squares, selector, packed, meta, rows, gate_up, spread, inner, out, *scratch
 ):
     total_scratch, gather_sems, (spread_send, spread_recv) = scratch[:9], scratch[9:13], scratch[13:15]
     (load, y_send, y_recv, right_send, right_recv, left_send, left_recv, far_send, far_recv, meta_send, meta_recv,
-     in_send, in_recv, on_send, on_recv, out_send, out_recv) = scratch[15:]
+     in_send, in_recv, on_send, on_recv, out_send, out_recv, share_send, share_recv) = scratch[15:34]
+    last_scratch = scratch[34:]
     tp, ep = lax.axis_index("tp"), lax.axis_index("ep")
     y, x = ep // RING, ep % RING
     z, core, chips, partner, z_right, z_left = tp_place()
     tokens, share = residual.shape
-    slots = back.shape[0] // RING // RING
+    slots = packed.shape[0] // RING
     width = weight.shape[1]
     block = RING * slots
     hidden_units = gate.shape[1]
@@ -205,8 +206,15 @@
         return (tp, ((y + dy + RING) % RING) * RING + (x + dx + RING) % RING)
 
     right, left = device(0, 1), device(0, -1)
+
+    def group_of(index):
+        return (index // RING - x + 2 + RING) % RING
+
+    owner = (x * RING + tp % RING, y * RING + (x - group_of(tp) + RING) % RING)
+    from_x = tp // RING
+    origin = ((2 * from_x - x + 2 + RING) % RING * RING + tp % RING, y * RING + from_x)
     greet(
-        [partner, z_right, z_left]
+        [partner, z_right, z_left, owner, origin]
         + [device(0, k) for k in range(1, RING)]
         + [device(k, 0) for k in range(1, RING)]
     )
@@ -286,6 +294,10 @@
         y_copies[d, g].wait_recv()
         to_sides(d, g, rows.at[chunk(0, d), group_columns(g)])
 
+    def gain_of(index):
+        lines = pair // 128
+        return jnp.concatenate([gain[pl.ds(index * lines + i, 1)] for i in range(lines)], axis=1)
+
     def dispatch(g):
         for p in GROUPS[g]:
             gather.ready(ORDER[p])
@@ -296,7 +308,7 @@
                 lanes = value[:, i * 128 : (i + 1) * 128]
                 total = total + lanes * lanes
             squares[...] = total
-            scaled = (value * gain[:, columns((z + ORDER[p]) % chips, pair)]).astype(BF16)
+            scaled = (value * gain_of((z + ORDER[p]) % chips)).astype(BF16)
             packed[:, part] = jnp.dot(selector[...], scaled, preferred_element_type=F32).astype(BF16)
         if g == len(GROUPS) - 1:
             mean = jnp.sum(squares[...], axis=1, keepdims=True) / width
@@ -397,27 +409,24 @@
     def gates():
         inverse = lax.rsqrt(jnp.sum(squares[...], axis=1, keepdims=True) / width + epsilon)
         count = router.shape[0]
-        logits = jnp.zeros((tokens, count), F32)
+        logits = jnp.zeros((count, tokens), F32)
         for p, j in enumerate(ORDER):
-            part = columns((z + j) % chips, pair)
-            normed = (hidden[:, pl.ds(p * pair, pair)].astype(F32) * inverse * gain[:, part]).astype(BF16)
+            index = (z + j) % chips
+            normed = (hidden[:, pl.ds(p * pair, pair)].astype(F32) * inverse * gain_of(index)).astype(BF16)
             logits = logits + lax.dot_general(
-                normed, router[:, part], (((1,), (1,)), ((), ())), preferred_element_type=F32
+                router[:, columns(index, pair)], normed, (((1,), (1,)), ((), ())), preferred_element_type=F32
             )
-        every = lax.broadcasted_iota(jnp.int32, (tokens, count), 1)
-        hit = every == ids[:, 0:1]
-        for k in range(1, ids.shape[1]):
-            hit = hit | (every == ids[:, k : k + 1])
-        top = jnp.max(jnp.where(hit, logits, -jnp.inf), axis=1, keepdims=True)
+        every = lax.broadcasted_iota(jnp.int32, (count, tokens), 0)
+        hit = every == ids[0:1]
+        for k in range(1, ids.shape[0]):
+            hit = hit | (every == ids[k : k + 1])
+        top = jnp.max(jnp.where(hit, logits, -jnp.inf), axis=0, keepdims=True)
         raised = jnp.where(hit, jnp.exp(jnp.where(hit, logits - top, 0.0)), 0.0)
-        softmax = raised / jnp.sum(raised, axis=1, keepdims=True)
-        lane = lax.broadcasted_iota(jnp.int32, (tokens, 128), 1)
-        own = jnp.zeros((tokens, 128), F32)
+        softmax = raised / jnp.sum(raised, axis=0, keepdims=True)
         for d in range(RING):
-            value = jnp.sum(jnp.where(every == tp * RING + (y + d) % RING, softmax, 0.0), axis=1, keepdims=True)
-            own = own + jnp.where(lane == d, value, 0.0)
+            own = every == tp * RING + (y + d) % RING
+            meta[pl.ds(RING + d, 1)] = jnp.sum(jnp.where(own, softmax, 0.0), axis=0, keepdims=True)
         meta[pl.ds(0, RING)] = places[pl.ds(0, RING)]
-        meta[pl.ds(RING, RING)] = own.T[:RING]
 
     gather.step(1)
     dispatch(0)
@@ -463,12 +472,12 @@
     onward(1, 0)
     came_left(2)
     onward(1, 1)
+    onward(2, 0)
+    onward(2, 1)
     relay(1, 0)
     relay(3, 0)
     came_far(0)
     unit(2, 0)
-    onward(2, 0)
-    onward(2, 1)
     unit(1, 1)
     unit(3, 1)
     relay(0, 1)
@@ -500,6 +509,31 @@
             remote(ref, ref, out_send.at[r, d], out_recv.at[r, d], device(d, 0)).wait_recv()
     for copy in metas:
         copy.wait_recv()
+    for r in range(RING):
+        for d in range(RING):
+            slot = meta_all[pl.ds(r * 2 * RING + d, 1)]
+            value = meta_all[pl.ds(r * 2 * RING + RING + d, 1)]
+            matrix[pl.ds((r * RING + PLACE[d]) * slots, slots)] = jnp.where(slot == place, value, 0.0).astype(BF16)
+
+    def mixed(index):
+        span = pl.ds(pl.multiple_of(group_of(index) * block, block), block)
+        return lax.dot_general(
+            matrix[span],
+            back[span, columns(index % RING, share)],
+            (((0,), (0,)), ((), ())),
+            preferred_element_type=F32,
+        )
+
+    def deliver(h, span, total):
+        share_out[span] = total.astype(BF16)
+        shares.append(
+            send(share_out.at[span], share_in.at[span], share_send.at[h], share_recv.at[h], owner)
+        )
+
+    shares = []
+    sum_over_tp(mixed, deliver, last_scratch)
+    for copy in shares:
+        copy.wait_recv()
     gather.finish()
     for copy in copies:
         copy.wait_send()
@@ -513,13 +547,16 @@
     return pl.pallas_call(
         layer_kernel,
         out_shape=(
-            jax.ShapeDtypeStruct((RING * total, width // RING), BF16),
-            jax.ShapeDtypeStruct((RING * 2 * RING, tokens), F32),
+            jax.ShapeDtypeStruct((tokens, share), BF16),
             jax.ShapeDtypeStruct((tokens, share), BF16),
         ),
         in_specs=in_vmem(7) + [pl.BlockSpec(memory_space=pl.ANY)] * 3,
-        out_specs=tuple(in_vmem(3)),
+        out_specs=tuple(in_vmem(2)),
         scratch_shapes=[
+            pltpu.VMEM((RING * total, width // RING), BF16),
+            pltpu.VMEM((RING * 2 * RING, tokens), F32),
+            pltpu.VMEM((RING * total, tokens), BF16),
+            pltpu.VMEM((tokens, share), BF16),
             pltpu.VMEM((tokens, width), BF16),
             pltpu.VMEM((tokens, 128), F32),
             pltpu.VMEM((total, tokens), BF16),
@@ -541,79 +578,14 @@
         + [dma((RING,))] * 2
         + [dma((RING, 3, RING))] * 2
         + [dma((RING, 3, 2))] * 2
-        + [dma((RING, RING))] * 2,
+        + [dma((RING, RING))] * 2
+        + [dma((2,))] * 2
+        + sum_scratch(tokens, share),
         compiler_params=pltpu.CompilerParams(
             collective_id=0, has_side_effects=True, vmem_limit_bytes=VMEM_BYTES
         ),
         name="layer",
     )(context, weight, residual, places, gain, router, ids, gate, up, down)
-
-
-def mix_kernel(meta, back, state, layer_out, share_out, share_in, matrix, share_send, share_recv, *scratch):
-    rows, width = state.shape
-    slots = back.shape[0] // RING // RING
-    tp, ep = lax.axis_index("tp"), lax.axis_index("ep")
-    y, x = ep // RING, ep % RING
-    z, core, chips, partner, right, left = tp_place()
-
-    def group_of(block):
-        return (block // RING - x + 2 + RING) % RING
-
-    target = (x * RING + tp % RING, y * RING + (x - group_of(tp) + RING) % RING)
-    from_x = tp // RING
-    shift = (from_x - x + RING) % RING
-    source = (((from_x + shift + 2) % RING) * RING + tp % RING, y * RING + from_x)
-    greet([partner, right, left, target, source])
-    place = lax.broadcasted_iota(jnp.int32, (slots, rows), 0).astype(F32)
-    for r in range(RING):
-        for d in range(RING):
-            slot = meta[pl.ds(r * 2 * RING + d, 1)]
-            gate = meta[pl.ds(r * 2 * RING + RING + d, 1)]
-            matrix[pl.ds((r * RING + PLACE[d]) * slots, slots)] = jnp.where(slot == place, gate, 0.0).astype(BF16)
-
-    def term(block):
-        span = pl.ds(pl.multiple_of(group_of(block) * RING * slots, RING * slots), RING * slots)
-        return lax.dot_general(
-            matrix[span],
-            back[span, columns(block % RING, width)],
-            (((0,), (0,)), ((), ())),
-            preferred_element_type=F32,
-        )
-
-    shares = []
-
-    def give(h, span, total):
-        share_out[span] = total.astype(BF16)
-        copy = remote(share_out.at[span], share_in.at[span], share_send.at[h], share_recv.at[h], target)
-        copy.start()
-        shares.append((span, copy))
-
-    sum_over_tp(term, give, scratch)
-    for span, copy in shares:
-        copy.wait()
-        layer_out[span] = (share_in[span].astype(F32) + state[span].astype(F32)).astype(BF16)
-
-
-def mix(meta, back, state):
-    rows, width = state.shape
-    return pl.pallas_call(
-        mix_kernel,
-        out_shape=jax.ShapeDtypeStruct((rows, width), BF16),
-        in_specs=in_vmem(3),
-        out_specs=pl.BlockSpec(memory_space=pltpu.VMEM),
-        scratch_shapes=[
-            pltpu.VMEM((rows, width), BF16),
-            pltpu.VMEM((rows, width), BF16),
-            pltpu.VMEM((back.shape[0], rows), BF16),
-            pltpu.SemaphoreType.DMA((2,)),
-            pltpu.SemaphoreType.DMA((2,)),
-        ]
-        + sum_scratch(rows, width),
-        compiler_params=pltpu.CompilerParams(
-            collective_id=1, has_side_effects=True, vmem_limit_bytes=VMEM_BYTES
-        ),
-        name="mix",
-    )(meta, back, state)
 
 
 def slots_of(expert_ids):
@@ -634,20 +606,20 @@
 ):
     rows = residual.shape[0]
     capacity = min(rows, 2 * rows * expert_ids.shape[1] // router_weight.shape[0])
-    back, meta_all, state = layer(
+    share, state = layer(
         context,
         out_weight,
         residual,
         slots_of(expert_ids),
-        norm_gain.astype(F32)[None],
+        norm_gain.astype(F32).reshape(-1, 128),
         router_weight,
-        expert_ids,
+        expert_ids.T,
         w_gate[0],
         w_up[0],
         w_down[0],
         capacity,
     )
-    return mix(meta_all, back, state)
+    return (share.astype(F32) + state.astype(F32)).astype(BF16)
 
 
 def solution(mesh):

time: 206 us -> 199 us (0.966)
  Pallas kernels: 197 us -> 192 us
  local copies, waits for them, and re-layouts: 3.05 us -> 0 us
    pallas_call x2 -> x1, Pallas kernels: 197 us -> 192 us  [layer(): pl.pallas_call(layer_kernel, out_shape=(jax.ShapeDtypeStruct((tokens, sha...]
    unnamed x2 -> x0, local copies, waits for them, and re-layouts: 3.05 us -> none
where the time goes in v6:
time: 199 us; the launch traced here: 196 us
  Pallas kernels  192 us (96%)
  other arithmetic  4.37 us (2%)
    pallas_call x1, Pallas kernels, layer(): pl.pallas_call(layer_kernel, out_shape=(jax.ShapeDtypeStruct((tokens, sha...  192 us

profile of v6, /device:TPU:32, one launch (start us, length us, event | category | flops | bytes accessed | tf_op | source)
XLA Modules:
  0.0 196.4 jit_solution(11295241990525164799)
XLA Ops:
  0.0 0.8 compare_reduce_fusion
  0.8 0.1 fusion
  0.9 0.6 pad_maximum_fusion.places
  1.6 1.3 bitcast_convert_fusion.gain
  2.9 191.9 %layer.1 = (bf16[256,256]{1,0:T(8,128)(2,1)}, bf16[256,256]{1,0:T(8,128)(2,1)}) custom-call(bf16[256,256]{1,0:T(8,128)(2,1)} %context.1, bf16[256,4096]{1,0:T(8,128)(2,1)} %weight.1, bf16[256,256]{1,0:T(8,128)(2,1)} %residual.1, f32[8,256]{1,0:T(8,128)} %pad_maximum_fusion.places, f32[32,128]{1,0:T(8,128)} %bitcast_convert_fusion.gain, ...), custom_call_target="tpu_custom_call" | custom-call | tf_op jit(solution)/shard_map/layer/pallas_call | solution.py:547
  194.7 1.7 add_convert_fusion
  (1 shorter events, 0.0 us)

commit v7 on v6

--- a/solution.py
+++ b/solution.py
@@ -454,12 +454,12 @@
     came_right(0)
     came_left(0)
     unit(0, 2)
-    for g in range(3):
-        y_arrived(2, g)
     came_right(1)
     onward(0, 0)
     came_left(3)
     onward(0, 1)
+    for g in range(3):
+        y_arrived(2, g)
     came_left(1)
     came_right(3)
     unit(1, 0)

time: 199 us -> 199 us (level)
  no operation moved by 1% of the time
where the time goes in v7:
time: 199 us; the launch traced here: 196 us
  Pallas kernels  192 us (96%)
  other arithmetic  4.37 us (2%)
    pallas_call x1, Pallas kernels, layer(): pl.pallas_call(layer_kernel, out_shape=(jax.ShapeDtypeStruct((tokens, sha...  192 us

profile of v7, /device:TPU:32, one launch (start us, length us, event | category | flops | bytes accessed | tf_op | source)
XLA Modules:
  0.0 196.4 jit_solution(6659312551810711915)
XLA Ops:
  0.0 0.8 compare_reduce_fusion
  0.8 0.1 fusion
  0.9 0.6 pad_maximum_fusion.places
  1.6 1.3 bitcast_convert_fusion.gain
  2.9 191.9 %layer.1 = (bf16[256,256]{1,0:T(8,128)(2,1)}, bf16[256,256]{1,0:T(8,128)(2,1)}) custom-call(bf16[256,256]{1,0:T(8,128)(2,1)} %context.1, bf16[256,4096]{1,0:T(8,128)(2,1)} %weight.1, bf16[256,256]{1,0:T(8,128)(2,1)} %residual.1, f32[8,256]{1,0:T(8,128)} %pad_maximum_fusion.places, f32[32,128]{1,0:T(8,128)} %bitcast_convert_fusion.gain, ...), custom_call_target="tpu_custom_call" | custom-call | tf_op jit(solution)/shard_map/layer/pallas_call | solution.py:547
  194.7 1.7 add_convert_fusion
  (1 shorter events, 0.0 us)
